TPU v7x, 32 devices: a whole 2x2x4 slice. The times are simulated.
32 devices in a mesh: grp: 2 (over x), sub: 16 (over z, y, core).
Axes of the slice: x: 2, y: 2, z: 4, core: 2. Of those that a mesh axis runs over, the one named last changes fastest.
Arguments:
- overall_quantity_unnormalized: float32 [16, 16, 256, 128], P(None, 'grp', 'sub'), may hold values from 0.05 to 1
- reservoir_pressure_field: float32 [16, 256, 128], P('grp', 'sub'), may hold values from 0.7 to 1.3
- reservoir_heat_level: float32 [16, 256, 128], P('grp', 'sub'), may hold values from 0.9 to 1.2
- condensed_flag: int32 [16, 256, 128], P('grp', 'sub'), may hold values 0 or 1
- permeability_field: float32 [16, 256, 128], P('grp', 'sub'), may hold values from 0.1 to 10
- pore_capacity: float32 [16, 256, 128], P('grp', 'sub'), may hold values from 0.05 to 0.3
- former_chemical_quantity: float32 [16, 16, 256, 128], P(None, 'grp', 'sub'), may hold values from 0 to 0.03
- transmissibility_multipliers: float32 [3], replicated, may hold values from 0.3 to 3
- viscosity_pair: float32 [2], replicated, may hold values from 0.3 to 3
- crit_kelvin_values: float32 [16], replicated, may hold values from 0.3 to 2.5
- attraction_parameters: float32 [16], replicated, may hold values from 0.3 to 4
- repulsive_parameters: float32 [16], replicated, may hold values from 0.02 to 0.15
- attraction_thermal_gradients: float32 [16], replicated, may hold values from 0.3 to 1.2
- binary_coupling_matrix: float32 [16, 16], replicated, may hold values from 0 to 0.3, as said below
- injected_recipe_unnormalized: float32 [16], replicated, may hold values from 0.05 to 1
- perforated_locale: int32 [8192], P(('grp', 'sub')), may hold values from 0 to 16383
- perforated_member: int32 [8192, 1], P(('grp', 'sub')), may hold values from 0 to 15; in each aligned block of 256 rows (0 to 255, 256 to 511, ...) at most 40 rows name the same one
- connection_conduit_piece: int32 [8192], P(('grp', 'sub')), may hold values from 0 to 31
- connection_inflow_strength: float32 [8192], P(('grp', 'sub')), may hold values from 0.02 to 0.2
- group_member_place: int32 [2, 16], P('grp'), may hold values from 0 to 15, each once within a row
- conduit_pieces_toe_forward: int32 [32, 32], P(('grp', 'sub')), may hold values from 0 to 31, each once within a row
- conduit_piece_pressures: float32 [32, 32], P(('grp', 'sub')), may hold values from 0.7 to 1.3
- downstream_exit_pressure: float32 [32], P(('grp', 'sub')), may hold values from 0.6 to 1.2
- friction_factors: float32 [32], P(('grp', 'sub')), may hold values from 3.0517578e-05 to 0.00030517578
Outputs:
- residual: float32 [16, 16, 256, 128], P(None, 'grp', 'sub')
- ln_phi: bfloat16 [16, 16, 256, 128], P(None, 'grp', 'sub')
- well_residual: float32 [32, 32], P(('grp', 'sub'))
Inputs may be any that keep to these rules, and one draw needn't show every extreme that they name: `perforated_locale`: flattened index (first, second, layer) of a cell of the listing device's own block. `perforated_member`: a well of the listing device's group; among the 256 rows of one device at most 40 name the same well. `group_member_place`: each row is a permutation; slot j of a group lies on the group's device j. `conduit_pieces_toe_forward`: each row is a permutation of the segments. `binary_coupling_matrix`: symmetric with zero diagonal.
All inputs are finite; a program needn't handle non-finite values. No bound on the sum of `condensed_flag` on one device may be relied on, other than what follows from the above.
Results may differ from a plain program's by a relative error of at most 0.001.
Values sent between devices are 32-bit elements; how exact they have to be, the bound alone decides.
No kernel may reach another device: no remote copies, remote signals or barrier semaphores. Data moves between devices by JAX's collectives and lax.ppermute only.
A program may use at most 64 MiB of HBM per device.

v0:
```python
import math

import jax
import jax.numpy as jnp
from jax import lax
from jax.sharding import PartitionSpec as P

NEWT = 8


ROOT_TWO = math.sqrt(2.0)


def extended(block, sides, width):
    for axis, dim in sides:
        count = lax.axis_size(axis)
        forward = [(i, i + 1) for i in range(count - 1)]
        backward = [(target, source) for source, target in forward]
        low = lax.ppermute(
            lax.slice_in_dim(block, block.shape[dim] - width, None, axis=dim), axis, forward
        )
        high = lax.ppermute(lax.slice_in_dim(block, 0, width, axis=dim), axis, backward)
        block = jnp.concatenate([low, block, high], axis=dim)
    return block


def gas_oil_partition(
    overall_quantity_unnormalized,
    reservoir_pressure_field,
    reservoir_heat_level,
    condensed_flag,
    crit_kelvin_values,
    attraction_parameters,
    repulsive_parameters,
    attraction_thermal_gradients,
    binary_coupling_matrix,
    viscosity_pair,
):
    shape = overall_quantity_unnormalized.shape
    replicate_across = (slice(None),) + (None,) * (len(shape) - 1)
    chemical_labels = overall_quantity_unnormalized / jnp.sum(overall_quantity_unnormalized, axis=0)
    thermal_adjuster = (
        1.0
        + attraction_thermal_gradients[replicate_across]
        * (1.0 - jnp.sqrt(reservoir_heat_level / crit_kelvin_values[replicate_across]))
    ) ** 2
    blended_attraction = (
        attraction_parameters[replicate_across]
        * thermal_adjuster
        * reservoir_pressure_field
        / (reservoir_heat_level * reservoir_heat_level)
    )
    roots = jnp.sqrt(blended_attraction)
    mixture_excluded_volume = (
        repulsive_parameters[replicate_across] * reservoir_pressure_field / reservoir_heat_level
    )
    mixed = jnp.dot(
        1.0 - binary_coupling_matrix,
        (roots * chemical_labels).reshape(shape[0], -1),
        precision=lax.Precision.HIGHEST,
    ).reshape(shape)
    psi = roots * mixed
    big_a = jnp.sum(chemical_labels * psi, axis=0)
    big_b = jnp.sum(chemical_labels * mixture_excluded_volume, axis=0)
    deviation_zvalue = jnp.where(condensed_flag == 1, big_b + 0.01, 1.0 + big_b)
    lin_c2 = big_b - 1.0
    lin_c1 = big_a - 3.0 * big_b * big_b - 2.0 * big_b
    lin_c0 = big_b * big_b + big_b * big_b * big_b - big_a * big_b
    for step in range(NEWT):
        value = (
            (deviation_zvalue + lin_c2) * deviation_zvalue + lin_c1
        ) * deviation_zvalue + lin_c0
        slope = (3.0 * deviation_zvalue + 2.0 * lin_c2) * deviation_zvalue + lin_c1
        deviation_zvalue = jnp.maximum(
            deviation_zvalue - value / jnp.maximum(slope, 0.1), big_b + 0.01
        )
    ratio = jnp.log(
        (deviation_zvalue + (1.0 + ROOT_TWO) * big_b)
        / (deviation_zvalue + (1.0 - ROOT_TWO) * big_b)
    )
    natural_log_activity = (
        mixture_excluded_volume / big_b * (deviation_zvalue - 1.0)
        - jnp.log(deviation_zvalue - big_b)
        - (
            psi / (ROOT_TWO * big_b)
            - big_a * mixture_excluded_volume / (2.0 * ROOT_TWO * big_b * big_b)
        )
        * ratio
    )
    blended_dilution_ratio = reservoir_pressure_field / (deviation_zvalue * reservoir_heat_level)
    visc = jnp.where(condensed_flag == 1, viscosity_pair[1], viscosity_pair[0])
    relative_flow_ease = blended_dilution_ratio / visc
    return (chemical_labels, natural_log_activity, blended_dilution_ratio, relative_flow_ease)


def face(c_a, p_a, k_a, c_b, p_b, k_b, factor):
    trans = factor * 2.0 * k_a * k_b / (k_a + k_b)
    return trans * (p_a - p_b) * jnp.where(p_a > p_b, c_a, c_b)


def layer_shift(arr, upward):
    width = [(0, 0)] * (arr.ndim - 1) + [(1, 1)]
    padded = jnp.pad(arr, width)
    if upward:
        return padded[..., 2:]
    return padded[..., :-2]


def all_fluxes(storage_term, carried_pad, press_pad, perm_pad, transmissibility_multipliers):
    c_a = carried_pad[:, 1:-1, 1:-1]
    p_a = press_pad[1:-1, 1:-1]
    k_a = perm_pad[1:-1, 1:-1]
    total = storage_term
    total = total + face(
        c_a,
        p_a,
        k_a,
        carried_pad[:, 2:, 1:-1],
        press_pad[2:, 1:-1],
        perm_pad[2:, 1:-1],
        transmissibility_multipliers[0],
    )
    total = total + face(
        c_a,
        p_a,
        k_a,
        carried_pad[:, :-2, 1:-1],
        press_pad[:-2, 1:-1],
        perm_pad[:-2, 1:-1],
        transmissibility_multipliers[0],
    )
    total = total + face(
        c_a,
        p_a,
        k_a,
        carried_pad[:, 1:-1, 2:],
        press_pad[1:-1, 2:],
        perm_pad[1:-1, 2:],
        transmissibility_multipliers[1],
    )
    total = total + face(
        c_a,
        p_a,
        k_a,
        carried_pad[:, 1:-1, :-2],
        press_pad[1:-1, :-2],
        perm_pad[1:-1, :-2],
        transmissibility_multipliers[1],
    )
    total = total + face(
        c_a,
        p_a,
        k_a,
        layer_shift(c_a, True),
        layer_shift(p_a, True),
        layer_shift(k_a, True),
        transmissibility_multipliers[2],
    )
    total = total + face(
        c_a,
        p_a,
        k_a,
        layer_shift(c_a, False),
        layer_shift(p_a, False),
        layer_shift(k_a, False),
        transmissibility_multipliers[2],
    )
    return total


def per_device(
    overall_quantity_unnormalized,
    reservoir_pressure_field,
    reservoir_heat_level,
    condensed_flag,
    permeability_field,
    pore_capacity,
    former_chemical_quantity,
    transmissibility_multipliers,
    viscosity_pair,
    crit_kelvin_values,
    attraction_parameters,
    repulsive_parameters,
    attraction_thermal_gradients,
    binary_coupling_matrix,
    injected_recipe_unnormalized,
    perforated_locale,
    perforated_member,
    connection_conduit_piece,
    connection_inflow_strength,
    group_member_place,
    conduit_pieces_toe_forward,
    conduit_piece_pressures,
    downstream_exit_pressure,
    friction_factors,
):
    ncomp = overall_quantity_unnormalized.shape[0]
    chemical_labels, natural_log_activity, blended_dilution_ratio, relative_flow_ease = (
        gas_oil_partition(
            overall_quantity_unnormalized,
            reservoir_pressure_field,
            reservoir_heat_level,
            condensed_flag,
            crit_kelvin_values,
            attraction_parameters,
            repulsive_parameters,
            attraction_thermal_gradients,
            binary_coupling_matrix,
            viscosity_pair,
        )
    )
    state = jnp.concatenate(
        [
            relative_flow_ease[None] * chemical_labels,
            reservoir_pressure_field[None],
            permeability_field[None],
        ],
        axis=0,
    )
    padded = extended(state, (("grp", 1), ("sub", 2)), 1)
    carried_pad = padded[:ncomp]
    press_pad = padded[ncomp]
    perm_pad = padded[ncomp + 1]
    storage_term = (
        pore_capacity * blended_dilution_ratio * chemical_labels - former_chemical_quantity
    )
    resid = all_fluxes(storage_term, carried_pad, press_pad, perm_pad, transmissibility_multipliers)
    block_shape = resid.shape
    p_flat = reservoir_pressure_field.reshape(-1)
    m_flat = relative_flow_ease.reshape(-1)
    z_flat = chemical_labels.reshape(ncomp, -1)
    p_cell = p_flat[perforated_locale]
    m_cell = m_flat[perforated_locale]
    z_cell = z_flat[:, perforated_locale]
    well_group = group_member_place.shape[1]
    well_slots = conduit_piece_pressures.shape[0]
    segments = conduit_piece_pressures.shape[1]
    perf_rows = perforated_locale.shape[0]
    owner_row = group_member_place[0]
    well_of = perforated_member[:, 0]
    well_hot = well_of[:, None] == jnp.arange(well_group, dtype=jnp.int32)[None, :]
    slot = jnp.sum(jnp.where(well_hot, owner_row[None, :], 0), axis=1)
    injected = injected_recipe_unnormalized / jnp.sum(injected_recipe_unnormalized)
    peers = lax.axis_size("sub")
    capacity = well_slots * max(2, 5 * perf_rows // (2 * well_group))
    dest = slot // well_slots
    dest_hot = (dest[:, None] == jnp.arange(peers, dtype=jnp.int32)[None, :]).astype(jnp.int32)
    before = jnp.cumsum(dest_hot, axis=0) - dest_hot
    position = jnp.sum(before * dest_hot, axis=1)
    target = dest * capacity + position
    place_hot = target[None, :] == jnp.arange(peers * capacity, dtype=jnp.int32)[:, None]
    place_float = place_hot.astype(jnp.float32)
    payload = jnp.concatenate(
        [z_cell, p_cell[None], m_cell[None], connection_inflow_strength[None]], axis=0
    )
    ints = jnp.stack([slot % well_slots, connection_conduit_piece], axis=0)
    packed = jnp.dot(payload, place_float.T, precision=lax.Precision.HIGHEST)
    send_float = jnp.swapaxes(packed.reshape(ncomp + 3, peers, capacity), 0, 1)
    packed_int = jnp.sum(jnp.where(place_hot[None], ints[:, None, :], 0), axis=2)
    send_int = jnp.swapaxes(packed_int.reshape(2, peers, capacity), 0, 1)
    local_table = conduit_piece_pressures.reshape(-1)
    got_float = lax.all_to_all(send_float, "sub", split_axis=0, concat_axis=0, tiled=True)
    got_int = lax.all_to_all(send_int, "sub", split_axis=0, concat_axis=0, tiled=True)
    random_keys = got_int[:, 0] * segments + got_int[:, 1]
    key_hot = random_keys[..., None] == jnp.arange(well_slots * segments, dtype=jnp.int32)
    p_seg = jnp.sum(jnp.where(key_hot, local_table, 0.0), axis=-1)
    drop = got_float[:, ncomp] - p_seg
    flow = (got_float[:, ncomp + 2] * got_float[:, ncomp + 1] * drop)[:, None, :] * jnp.where(
        drop[:, None, :] > 0, got_float[:, :ncomp], injected[None, :, None]
    )
    totals = jnp.sum(flow, axis=1)
    seg_part = jnp.swapaxes(jnp.where(key_hot, totals[..., None], 0.0), 1, 2)
    returned = lax.all_to_all(flow, "sub", split_axis=0, concat_axis=0, tiled=True)
    returned, seg_part = (returned, seg_part)
    flat_back = jnp.swapaxes(returned, 0, 1).reshape(ncomp, peers * capacity)
    inflow = jnp.dot(flat_back, place_float, precision=lax.Precision.HIGHEST)
    rate = jnp.sum(seg_part, axis=(0, 2)).reshape(well_slots, segments)
    resid_flat = resid.reshape(ncomp, -1).at[:, perforated_locale].add(inflow)
    residual = resid_flat.reshape(block_shape)
    order_hot = (
        conduit_pieces_toe_forward[:, :, None] == jnp.arange(segments)[None, None, :]
    ).astype(jnp.float32)
    ordered = jnp.einsum("wks,ws->wk", order_hot, rate, precision=lax.Precision.HIGHEST)
    upper = (jnp.arange(segments)[:, None] <= jnp.arange(segments)[None, :]).astype(jnp.float32)
    running = jnp.dot(ordered, upper, precision=lax.Precision.HIGHEST)
    press_ord = jnp.einsum(
        "wks,ws->wk", order_hot, conduit_piece_pressures, precision=lax.Precision.HIGHEST
    )
    nexts = jnp.concatenate([press_ord[:, 1:], downstream_exit_pressure[:, None]], axis=1)
    res_ord = press_ord - nexts - friction_factors[:, None] * running * jnp.abs(running)
    well_residual = jnp.einsum("wks,wk->ws", order_hot, res_ord, precision=lax.Precision.HIGHEST)
    return (residual, natural_log_activity.astype(jnp.bfloat16), well_residual)


def solution(mesh):
    in_specs = (
        P(None, "grp", "sub", None),
        P("grp", "sub", None),
        P("grp", "sub", None),
        P("grp", "sub", None),
        P("grp", "sub", None),
        P("grp", "sub", None),
        P(None, "grp", "sub", None),
        P(),
        P(),
        P(),
        P(),
        P(),
        P(),
        P(),
        P(),
        P(("grp", "sub")),
        P(("grp", "sub"), None),
        P(("grp", "sub")),
        P(("grp", "sub")),
        P("grp", None),
        P(("grp", "sub"), None),
        P(("grp", "sub"), None),
        P(("grp", "sub")),
        P(("grp", "sub")),
    )
    out_specs = (P(None, "grp", "sub", None), P(None, "grp", "sub", None), P(("grp", "sub"), None))
    return jax.shard_map(
        per_device, mesh=mesh, in_specs=in_specs, out_specs=out_specs, check_vma=False
    )
```

profile of v0, /device:TPU:10, one launch (start us, length us, event | category | flops | bytes accessed | tf_op | source)
XLA Modules:
  0.0 110.3 jit_solution(4548528352154858279)
XLA Ops:
  0.7 0.8 select_reduce_fusion.3
  1.6 0.7 stack.8
  2.2 0.6 reduce-window.6
  3.3 0.5 copy-done.11
  4.1 0.6 copy.98
  4.7 6.3 %all-to-all-start.1 = ((s32[16,2,40]{2,1,0:T(2,128)}), s32[16,2,40]{2,1,0:T(2,128)S(1)}, u32[]{:S(2)}, u32[]{:S(2)}) async-start(s32[16,2,40]{2,1,0:T(2,128)} %copy.98), calls=%async_computation.1 | async-start | bytes 32768 | tf_op jit(solution)/shard_map/all_to_all | solution.py:263
  11.0 1.3 %fusion.143 = (f32[1]{0:T(128)}, f32[1]{0:T(128)}) fusion(f32[2]{0:T(128)} %param.32), kind=kLoop, calls=%fused_computation.256 | loop fusion | bytes 16 | tf_op jit(solution)/shard_map/slice | solution.py:91
  12.3 0.9 mul.456
  13.3 1.3 %reduce_sum.92 = f32[8,16,128]{2,1,0:T(8,128)S(1)} reduce(f32[16,8,16,128]{3,2,1,0:T(8,128)} %param.24, f32[]{:T(128)} %constant.55.clone.1), dimensions={0}, to_apply=%region_0.0 | reduce | flops 245760 | bytes 1114116 | tf_op jit(solution)/shard_map/reduce_sum | solution.py:41
  14.6 2.5 %fusion.31 = (f32[16,8,16,128]{3,0,2,1:T(8,128)S(1)}, f32[16,8,16,128]{3,0,2,1:T(8,128)S(1)}) fusion(f32[8,16,128]{2,1,0:T(8,128)S(1)} %mul.456, f32[8,16,128]{2,1,0:T(8,128)} %param.25, f32[16]{0:T(128)} %param.33, f32[8,16,128]{2,1,0:T(8,128)} %param.26, f32[16]{0:T(128)} %param.36, f32[16]{0:T(128)} %param.34, f32[8,16,128]{2,1,0:T(8,128)S(1)} %reduce_sum.92, ...), kind=kLoop, calls=%fused_computation.67 | loop fusion | flops 2621440 | bytes 3408064 | tf_op jit(solution)/shard_map/mul | solution.py:59
  17.4 0.6 copy.132
  18.4 2.6 %multiply_reduce_fusion = (f32[8,16,128]{2,1,0:T(8,128)S(1)}, f32[8,16,128]{2,1,0:T(8,128)S(1)}, f32[16,8,16,128]{3,0,2,1:T(8,128)S(1)}) fusion(f32[16,8,16,128]{3,0,2,1:T(8,128)S(1)} %get-tuple-element.26, f32[8,16,128]{2,1,0:T(8,128)S(1)} %copy-done.1, f32[8,16,128]{2,1,0:T(8,128)S(1)} %copy-done, f32[16]{0:T(128)S(1)} %copy-done.13, ...), kind=kOutput, calls=%fused_computation.62 | convolution fusion | flops 54231296 | bytes 3474688 | tf_op jit(solution)/shard_map/dot_general | solution.py:57
  21.4 1.4 %subtract_log_fusion = (f32[8,16,128]{2,1,0:T(8,128)S(1)}, f32[8,16,128]{2,1,0:T(8,128)S(1)}, f32[8,16,128]{2,1,0:T(8,128)S(1)}, f32[8,16,128]{2,1,0:T(8,128)S(1)}) fusion(f32[8,16,128]{2,1,0:T(8,128)S(1)} %get-tuple-element.55, f32[8,16,128]{2,1,0:T(8,128)S(1)} %get-tuple-element.19, f32[8,16,128]{2,1,0:T(8,128)S(1)} %copy-done, ...), kind=kLoop, calls=%fused_computation.163 | loop fusion | flops 196608 | bytes 606216 | tf_op jit(solution)/shard_map/log | solution.py:83
  22.8 0.8 fusion.30
  23.6 0.8 pad_maximum_fusion.18
  24.4 1.3 %collective-permute-start = (f32[18,1,16,128]{3,0,2,1:T(8,128)}, f32[18,1,16,128]{3,0,2,1:T(8,128)S(1)}, u32[]{:S(2)}, u32[]{:S(2)}) collective-permute-start(f32[18,1,16,128]{3,0,2,1:T(8,128)} %get-tuple-element.31), channel_id=1, source_target_pairs={{0,16},{1,17},{2,18},{3,19},{4,20},{5,21},{6,22},{7,23},{8,24},{9,... | collective-permute-start | bytes 442376 | tf_op jit(solution)/shard_map/ppermute | solution.py:19
  25.7 4.6 %collective-permute-start.1 = (f32[18,1,16,128]{3,0,2,1:T(8,128)}, f32[18,1,16,128]{3,0,2,1:T(8,128)S(1)}, u32[]{:S(2)}, u32[]{:S(2)}) collective-permute-start(f32[18,1,16,128]{3,0,2,1:T(8,128)} %get-tuple-element.32), channel_id=1, source_target_pairs={{16,0},{17,1},{18,2},{19,3},{20,4},{21,5},{22,6},{23,7},{24,8},{25... | collective-permute-start | bytes 442376 | tf_op jit(solution)/shard_map/ppermute | solution.py:22
  30.3 4.6 %copy.107 = f32[16,8,16,128]{0,3,2,1:T(8,128)} copy(f32[16,8,16,128]{3,0,2,1:T(8,128)S(1)} %get-tuple-element.26) | data formatting | bytes 2097152 | tf_op jit(solution)/shard_map/reshape | solution.py:231
  34.9 1.3 %reduce_sum.100 = f32[]{:T(128)} reduce(f32[16]{0:T(128)} %param.38, f32[]{:T(128)} %constant.55.clone.1), dimensions={0}, to_apply=%region_9.10 | reduce | flops 15 | bytes 72 | tf_op jit(solution)/shard_map/reduce_sum | solution.py:243
  36.1 1.8 %broadcast_divide_fusion = f32[16]{0:T(128)} fusion(f32[16]{0:T(128)} %param.38, f32[]{:T(128)} %reduce_sum.100), kind=kLoop, calls=%fused_computation.249 | loop fusion | flops 16 | bytes 132 | tf_op jit(solution)/shard_map/div | solution.py:243
  38.0 0.9 fusion.123
  38.8 0.6 slice_bitcast_fusion
  39.4 0.7 compare_select_fusion
  40.1 1.7 %gather_fusion.1 = f32[256]{0:T(256)S(1)} fusion(f32[16384]{0:T(1024)S(1)} %bitcast.119, s32[1024]{0:T(1024)S(1)} %pad_clamp_fusion), kind=kCustom, calls=%fused_computation.1 | custom fusion | bytes 3072 | tf_op jit(solution)/shard_map/gather | solution.py:232
  41.9 1.7 %gather_fusion.2 = f32[256]{0:T(256)S(1)} fusion(f32[16384]{0:T(1024)S(1)} %bitcast.125, s32[1024]{0:T(1024)S(1)} %pad_clamp_fusion), kind=kCustom, calls=%fused_computation.2 | custom fusion | bytes 3072 | tf_op jit(solution)/shard_map/gather | solution.py:233
  43.6 4.1 %gather_fusion = f32[256,16]{1,0:T(8,128)S(1)} fusion(f32[16,16384]{0,1:T(8,128)} %bitcast.126, s32[1024]{0:T(1024)S(1)} %pad_clamp_fusion), kind=kCustom, calls=%fused_computation | custom fusion | bytes 33792 | tf_op jit(solution)/shard_map/gather | solution.py:234
  48.2 0.6 fusion.142
  51.9 0.9 copy.103
  53.1 0.8 reshape.279
  53.9 6.0 %all-to-all-start = ((f32[16,1,760]{2,1,0:T(1,128)}), f32[16,1,760]{2,1,0:T(1,128)S(1)}, u32[]{:S(2)}, u32[]{:S(2)}) async-start(f32[16,1,760]{2,1,0:T(1,128)} %reshape.279), calls=%async_computation | async-start | bytes 98304 | tf_op jit(solution)/shard_map/all_to_all | solution.py:262
  60.0 4.9 %all-to-all-done = f32[16,1,760]{2,1,0:T(1,128)S(1)} async-done(((f32[16,1,760]{2,1,0:T(1,128)}), f32[16,1,760]{2,1,0:T(1,128)S(1)}, u32[]{:S(2)}, u32[]{:S(2)}) %all-to-all-start) | async-done | bytes 48672 | tf_op jit(solution)/shard_map/all_to_all | solution.py:262
  65.0 0.6 broadcast.223
  65.5 0.8 reduce.3
  66.5 0.7 fusion.137
  67.4 0.8 convolution_bitcast_fusion.1
  68.2 0.8 reshape.281
  69.0 5.1 %all-to-all-start.2 = ((f32[16,1,640]{2,1,0:T(1,128)}), f32[16,1,640]{2,1,0:T(1,128)S(1)}, u32[]{:S(2)}, u32[]{:S(2)}) async-start(f32[16,1,640]{2,1,0:T(1,128)} %reshape.281), calls=%async_computation.2 | async-start | bytes 81920 | tf_op jit(solution)/shard_map/all_to_all | solution.py:273
  74.1 0.7 fusion.132
  74.9 1.4 %fusion.120 = f32[1,32]{1,0:T(1,128)} fusion(f32[32,1]{0,1:T(1,128)S(1)} %fusion.132, s32[32]{0:T(128)} %bitcast.157), kind=kOutput, calls=%fused_computation.220 | convolution fusion | flops 13312 | bytes 384 | tf_op jit(solution)/shard_map/wks,wk->ws/dot_general | solution.py:291
  76.3 3.1 %collective-permute-start.3 = (f32[18,10,1,128]{3,0,2,1:T(8,128)S(1)}, f32[18,10,1,128]{3,0,2,1:T(8,128)S(1)}, u32[]{:S(2)}, u32[]{:S(2)}) collective-permute-start(f32[18,10,1,128]{3,0,2,1:T(8,128)S(1)} %get-tuple-element.29), channel_id=1, source_target_pairs={{1,0},{2,1},{3,2},{4,3},{5,4},{6,5},{7,6},{8,7},{9,8},{10,9},{11,1... | collective-permute-start | bytes 276488 | tf_op jit(solution)/shard_map/ppermute | solution.py:22
  79.4 2.1 %collective-permute-start.2 = (f32[18,10,1,128]{3,0,2,1:T(8,128)S(1)}, f32[18,10,1,128]{3,0,2,1:T(8,128)S(1)}, u32[]{:S(2)}, u32[]{:S(2)}) collective-permute-start(f32[18,10,1,128]{3,0,2,1:T(8,128)S(1)} %get-tuple-element.30), channel_id=1, source_target_pairs={{0,1},{1,2},{2,3},{3,4},{4,5},{5,6},{6,7},{7,8},{8,9},{9,10},{10,1... | collective-permute-start | bytes 276488 | tf_op jit(solution)/shard_map/ppermute | solution.py:19
  81.5 0.8 reduce.4
  82.6 1.8 %fusion.34 = f32[256,16]{1,0:T(8,128)} fusion(f32[16,640]{1,0:T(8,128)S(1)} %reshape.231, s32[256]{0:T(256)} %copy-done.11), kind=kOutput, calls=%fused_computation.70 | convolution fusion | flops 31784960 | bytes 58368 | tf_op jit(solution)/shard_map/dot_general | solution.py:276
  84.4 2.1 %collective-permute-done.2 = f32[18,10,1,128]{3,0,2,1:T(8,128)S(1)} collective-permute-done((f32[18,10,1,128]{3,0,2,1:T(8,128)S(1)}, f32[18,10,1,128]{3,0,2,1:T(8,128)S(1)}, u32[]{:S(2)}, u32[]{:S(2)}) %collective-permute-start.2) | collective-permute-done | bytes 92192 | tf_op jit(solution)/shard_map/ppermute | solution.py:19
  87.2 3.7 %fusion.14 = f32[16,8,16,128]{3,0,2,1:T(8,128)S(1)} fusion(f32[16,8,16,128]{3,0,2,1:T(8,128)S(1)} %get-tuple-element.68, f32[18,10,1,128]{3,0,2,1:T(8,128)} %copy-done.5, f32[18,1,16,128]{3,0,2,1:T(8,128)} %copy-done.2, f32[18,1,16,128]{3,0,2,1:T(8,128)S(1)} %collective-permute-done, f32[1,8,16,128]{3,0,2,1:T(1,128)S(1)} %bitcast.135, ...), kind=kLoop, calls=%fused_computation.27 | loop fusion | flops 9437184 | bytes 5361664 | tf_op jit(solution)/shard_map/add | solution.py:159
  90.9 4.6 %copy.106 = f32[16,8,16,128]{0,3,2,1:T(8,128)} copy(f32[16,8,16,128]{3,0,2,1:T(8,128)S(1)} %fusion.14) | data formatting | bytes 2097152 | tf_op jit(solution)/shard_map/reshape | solution.py:278
  95.5 8.7 %scatter_fusion = f32[16,16384]{0,1:T(8,128)} fusion(f32[16,16384]{0,1:T(8,128)} %bitcast.123, s32[256]{0:T(256)S(1)} %copy-done.9, f32[256,16]{1,0:T(8,128)} %fusion.34), kind=kCustom, calls=%fused_computation.3 | custom fusion | flops 4096 | bytes 50176 | tf_op jit(solution)/shard_map/scatter-add | solution.py:278
  104.3 6.1 %copy.102 = f32[16,8,16,128]{3,2,1,0:T(8,128)} copy(f32[16,8,16,128]{0,3,2,1:T(8,128)} %bitcast.124) | data formatting | bytes 2097152
  (84 shorter events, 3.9 us)
Async XLA Ops:
  0.6 17.7 %copy-start.1 = (f32[8,16,128]{2,1,0:T(8,128)S(1)}, f32[8,16,128]{2,1,0:T(8,128)}, u32[]{:S(2)}) copy-start(f32[8,16,128]{2,1,0:T(8,128)} %param.26) | copy-start | bytes 196612
  0.6 17.7 %copy-start = (f32[8,16,128]{2,1,0:T(8,128)S(1)}, f32[8,16,128]{2,1,0:T(8,128)}, u32[]{:S(2)}) copy-start(f32[8,16,128]{2,1,0:T(8,128)} %param.25) | copy-start | bytes 196612
  0.7 17.7 %copy-start.17 = (f32[16]{0:T(128)S(1)}, f32[16]{0:T(128)}, u32[]{:S(2)}) copy-start(f32[16]{0:T(128)} %param.36) | copy-start | bytes 196
  0.7 17.7 %copy-start.18 = (f32[16]{0:T(128)S(1)}, f32[16]{0:T(128)}, u32[]{:S(2)}) copy-start(f32[16]{0:T(128)} %param.34) | copy-start | bytes 196
  0.7 17.6 %copy-start.16 = (f32[16]{0:T(128)S(1)}, f32[16]{0:T(128)}, u32[]{:S(2)}) copy-start(f32[16]{0:T(128)} %param.33) | copy-start | bytes 196
  0.7 17.6 %copy-start.13 = (f32[16]{0:T(128)S(1)}, f32[16]{0:T(128)}, u32[]{:S(2)}) copy-start(f32[16]{0:T(128)} %param.35) | copy-start | bytes 196
  0.7 17.6 %copy-start.19 = (f32[16,16]{1,0:T(8,128)S(1)}, f32[16,16]{1,0:T(8,128)}, u32[]{:S(2)}) copy-start(f32[16,16]{1,0:T(8,128)} %param.37) | copy-start | bytes 3076
  3.1 0.6 copy-start.11
  4.7 49.1 %all-to-all-start.1 = ((s32[16,2,40]{2,1,0:T(2,128)}), s32[16,2,40]{2,1,0:T(2,128)S(1)}, u32[]{:S(2)}, u32[]{:S(2)}) async-start(s32[16,2,40]{2,1,0:T(2,128)} %copy.98), calls=%async_computation.1 | async-start | bytes 32768 | tf_op jit(solution)/shard_map/all_to_all | solution.py:263
  18.0 3.0 %copy-start.6 = (s32[8,16,128]{2,1,0:T(8,128)S(1)}, s32[8,16,128]{2,1,0:T(8,128)}, u32[]{:S(2)}) copy-start(s32[8,16,128]{2,1,0:T(8,128)} %param.27) | copy-start | bytes 196612
  18.0 3.3 %copy-start.7 = (f32[8,16,128]{2,1,0:T(8,128)S(1)}, f32[8,16,128]{2,1,0:T(8,128)}, u32[]{:S(2)}) copy-start(f32[8,16,128]{2,1,0:T(8,128)} %param.29) | copy-start | bytes 196612
  18.1 4.7 %copy-start.14 = (f32[16]{0:T(128)S(1)}, f32[16]{0:T(128)}, u32[]{:S(2)}) copy-start(f32[16]{0:T(128)} %param.35) | copy-start | bytes 196
  18.4 5.3 %copy-start.3 = (f32[8,16,128]{2,1,0:T(8,128)S(1)}, f32[8,16,128]{2,1,0:T(8,128)}, u32[]{:S(2)}) copy-start(f32[8,16,128]{2,1,0:T(8,128)} %param.28) | copy-start | bytes 196612
  22.8 25.0 %copy-start.12 = (s32[256]{0:T(256)S(1)}, s32[256]{0:T(256)}, u32[]{:S(2)}) copy-start(s32[256]{0:T(256)} %copy-done.11) | copy-start | bytes 3076
  22.8 25.0 %copy-start.20 = (f32[256]{0:T(256)S(1)}, f32[256]{0:T(256)}, u32[]{:S(2)}) copy-start(f32[256]{0:T(256)} %param.42) | copy-start | bytes 3076
  22.8 25.4 %copy-start.10 = (f32[3]{0:T(128)S(1)}, f32[3]{0:T(128)}, u32[]{:S(2)}) copy-start(f32[3]{0:T(128)} %param.31) | copy-start | bytes 40
  23.6 36.3 %copy-start.15 = (f32[1,32]{1,0:T(1,128)S(1)}, f32[1,32]{1,0:T(1,128)}, u32[]{:S(2)}) copy-start(f32[1,32]{1,0:T(1,128)} %param.45) | copy-start | bytes 388
  24.4 51.8 %collective-permute-start = (f32[18,1,16,128]{3,0,2,1:T(8,128)}, f32[18,1,16,128]{3,0,2,1:T(8,128)S(1)}, u32[]{:S(2)}, u32[]{:S(2)}) collective-permute-start(f32[18,1,16,128]{3,0,2,1:T(8,128)} %get-tuple-element.31), channel_id=1, source_target_pairs={{0,16},{1,17},{2,18},{3,19},{4,20},{5,21},{6,22},{7,23},{8,24},{9,... | collective-permute-start | bytes 442376 | tf_op jit(solution)/shard_map/ppermute | solution.py:19
  25.7 50.5 %collective-permute-start.1 = (f32[18,1,16,128]{3,0,2,1:T(8,128)}, f32[18,1,16,128]{3,0,2,1:T(8,128)S(1)}, u32[]{:S(2)}, u32[]{:S(2)}) collective-permute-start(f32[18,1,16,128]{3,0,2,1:T(8,128)} %get-tuple-element.32), channel_id=1, source_target_pairs={{16,0},{17,1},{18,2},{19,3},{20,4},{21,5},{22,6},{23,7},{24,8},{25... | collective-permute-start | bytes 442376 | tf_op jit(solution)/shard_map/ppermute | solution.py:22
  38.8 1.3 %copy-start.21 = (f32[1,32]{1,0:T(1,128)}, f32[1,32]{1,0:T(1,128)S(1)}, u32[]{:S(2)}) copy-start(f32[1,32]{1,0:T(1,128)S(1)} %fusion.123) | copy-start | bytes 388
  40.1 7.6 %copy-start.8 = (s32[256]{0:T(256)}, s32[256]{0:T(256)S(1)}, u32[]{:S(2)}) copy-start(s32[256]{0:T(256)S(1)} %compare_select_fusion) | copy-start | bytes 3076
  53.9 11.1 %all-to-all-start = ((f32[16,1,760]{2,1,0:T(1,128)}), f32[16,1,760]{2,1,0:T(1,128)S(1)}, u32[]{:S(2)}, u32[]{:S(2)}) async-start(f32[16,1,760]{2,1,0:T(1,128)} %reshape.279), calls=%async_computation | async-start | bytes 98304 | tf_op jit(solution)/shard_map/all_to_all | solution.py:262
  69.0 12.5 %all-to-all-start.2 = ((f32[16,1,640]{2,1,0:T(1,128)}), f32[16,1,640]{2,1,0:T(1,128)S(1)}, u32[]{:S(2)}, u32[]{:S(2)}) async-start(f32[16,1,640]{2,1,0:T(1,128)} %reshape.281), calls=%async_computation.2 | async-start | bytes 81920 | tf_op jit(solution)/shard_map/all_to_all | solution.py:273
  76.2 10.9 %copy-start.2 = (f32[18,1,16,128]{3,0,2,1:T(8,128)}, f32[18,1,16,128]{3,0,2,1:T(8,128)S(1)}, u32[]{:S(2)}) copy-start(f32[18,1,16,128]{3,0,2,1:T(8,128)S(1)} %collective-permute-done.1) | copy-start | bytes 442372
  76.3 8.1 %collective-permute-start.3 = (f32[18,10,1,128]{3,0,2,1:T(8,128)S(1)}, f32[18,10,1,128]{3,0,2,1:T(8,128)S(1)}, u32[]{:S(2)}, u32[]{:S(2)}) collective-permute-start(f32[18,10,1,128]{3,0,2,1:T(8,128)S(1)} %get-tuple-element.29), channel_id=1, source_target_pairs={{1,0},{2,1},{3,2},{4,3},{5,4},{6,5},{7,6},{8,7},{9,8},{10,9},{11,1... | collective-permute-start | bytes 276488 | tf_op jit(solution)/shard_map/ppermute | solution.py:22
  79.4 7.1 %collective-permute-start.2 = (f32[18,10,1,128]{3,0,2,1:T(8,128)S(1)}, f32[18,10,1,128]{3,0,2,1:T(8,128)S(1)}, u32[]{:S(2)}, u32[]{:S(2)}) collective-permute-start(f32[18,10,1,128]{3,0,2,1:T(8,128)S(1)} %get-tuple-element.30), channel_id=1, source_target_pairs={{0,1},{1,2},{2,3},{3,4},{4,5},{5,6},{6,7},{7,8},{8,9},{9,10},{10,1... | collective-permute-start | bytes 276488 | tf_op jit(solution)/shard_map/ppermute | solution.py:19
  84.4 2.8 %copy-start.4 = (f32[18,10,1,128]{3,0,2,1:T(8,128)}, f32[18,10,1,128]{3,0,2,1:T(8,128)S(1)}, u32[]{:S(2)}) copy-start(f32[18,10,1,128]{3,0,2,1:T(8,128)S(1)} %collective-permute-done.3) | copy-start | bytes 276484
  86.5 0.7 copy-start.5
  86.8 8.8 %copy-start.9 = (s32[256]{0:T(256)S(1)}, s32[256]{0:T(256)}, u32[]{:S(2)}) copy-start(s32[256]{0:T(256)} %copy-done.8) | copy-start | bytes 3076
where the time goes:
time: 111 us; the launch traced here: 110 us
  local copies, waits for them, and re-layouts  32.4 us (29%)
  other arithmetic  29.4 us (26%)
  starting transfers between devices  28.5 us (26%)
  matrix products  8.68 us (8%)
  waiting for transfers between devices  7.03 us (6%)
  between operations  4.36 us (4%)
    unnamed x54, local copies, waits for them, and re-layouts  10.2 us
    scatter-add x1, other arithmetic, per_device(): resid_flat = resid.reshape(ncomp, -1).at[:, perforated_locale].add(inflow)  8.72 us
    ppermute x2, starting transfers between devices, extended(): lax.ppermute(lax.slice_in_dim(block, 0, width, axis=dim), axis, backward)  7.67 us
    all_to_all x1, starting transfers between devices, per_device(): lax.all_to_all(send_int, 'sub', split_axis=0, concat_axis=0, tiled=True)  6.3 us
    all_to_all x1, starting transfers between devices, per_device(): lax.all_to_all(send_float, 'sub', split_axis=0, concat_axis=0, tiled=True)  6.02 us
    all_to_all x1, starting transfers between devices, per_device(): lax.all_to_all(flow, 'sub', split_axis=0, concat_axis=0, tiled=True)  5.08 us
    all_to_all x1, waiting for transfers between devices, per_device(): lax.all_to_all(send_float, 'sub', split_axis=0, concat_axis=0, tiled=True)  4.92 us
    reshape x1, local copies, waits for them, and re-layouts, per_device(): z_flat = chemical_labels.reshape(ncomp, -1)  4.61 us
  transfers between devices with their start and end apart: 7, of which 2 were waited for; matrix products, arithmetic and copies ran while one was open for 39% of the time, Pallas kernels for 0%

commit v1 on v0

v1 whole, which is shorter than its diff:
```python
import functools
import math

import jax
import jax.numpy as jnp
from jax import lax
from jax.experimental import pallas as pl
from jax.experimental.pallas import tpu as pltpu
from jax.sharding import PartitionSpec as P

NEWT = 8
ROOT_TWO = math.sqrt(2.0)
LANES = 128
SUBLANES = 8
F32 = jnp.float32
BF16 = jnp.bfloat16
VMEM_LIMIT = 48 * 1024 * 1024
MARGIN = 8


def iota(shape, dim):
    return lax.broadcasted_iota(jnp.int32, shape, dim)


def pieces_of(x, count):
    out = []
    for _ in range(count):
        piece = x.astype(BF16)
        out.append(piece)
        x = x - piece.astype(F32)
    return out


def mat(a, b):
    return lax.dot_general(a, b, (((1,), (0,)), ((), ())), preferred_element_type=F32)


def mat_nt(a, b):
    return lax.dot_general(a, b, (((1,), (1,)), ((), ())), preferred_element_type=F32)


def mat_hot(x, hot, count=3):
    return sum(mat(piece, hot) for piece in pieces_of(x, count))


def hot_mat_nt(hot, x, count=3):
    return sum(mat_nt(hot, piece) for piece in pieces_of(x, count))


def hot(cond):
    return jnp.where(cond, 1.0, 0.0).astype(BF16)


def place_hots(loc, rows):
    n = loc.shape[1]
    row_hot = iota((rows, n), 0) == loc // LANES
    lane_hot = iota((LANES, n), 0) == loc % LANES
    return row_hot, lane_hot


def slot_hot_of(member, place):
    wells = place.shape[1]
    slot_of = hot(iota((wells, wells), 0) == place)
    member_hot = hot(iota((wells, member.shape[1]), 0) == member)
    return mat(slot_of, member_hot)


def phase_kernel(
    nx,
    ny,
    axes,
    amount,
    press,
    heat,
    flag,
    perm,
    visc,
    crit,
    attract,
    covol,
    slope,
    coupling,
    loc,
    member,
    seg,
    strength,
    place,
    lnphi_out,
    carried_out,
    mob_out,
    edge_x_out,
    edge_ya_out,
    edge_yb_out,
    part_out,
    pcell_out,
    amount_v,
    split_v,
    psi_v,
    carried_v,
    lnphi_v,
    field_v,
    table_v,
    in_sems,
    out_sems,
    edge_sem,
):
    nc = amount.shape[0]
    per = 2
    chunks = nx // per
    rows = per * ny
    loads = []
    for c in range(chunks):
        span = pl.ds(c * rows, rows)
        copy = pltpu.make_async_copy(amount.at[:, span], amount_v.at[:, span], in_sems.at[c])
        copy.start()
        loads.append(copy)

    for i in range(nc):
        root = jnp.sqrt(jnp.full((SUBLANES, LANES), attract[i], F32))
        kappa = jnp.full((SUBLANES, LANES), slope[i], F32)
        tc = jnp.full((SUBLANES, LANES), crit[i], F32)
        table_v[0, i] = root * (1.0 + kappa)
        table_v[1, i] = root * kappa / jnp.sqrt(tc)
        table_v[2, i] = jnp.full((SUBLANES, LANES), covol[i], F32)

    size = nc * ny
    spread = hot(iota((size, nc), 0) // ny == iota((size, nc), 1))
    same_row = iota((size, size), 0) % ny == iota((size, size), 1) % ny
    mixers = []
    for piece in pieces_of(1.0 - coupling[...], 2):
        wide = mat(spread, piece).astype(BF16)
        mixers.append(jnp.where(same_row, mat_nt(wide, spread), 0.0).astype(BF16))
    mixer = jnp.concatenate([mixers[0], mixers[0], mixers[1]], axis=1)

    shape3 = (ny // SUBLANES, SUBLANES, LANES)
    stores = []
    half = chunks // 2
    for h in range(2):
        for c in range(h * half, (h + 1) * half):
            loads[c].wait()
            for x in range(c * per, (c + 1) * per):
                span = pl.ds(x * ny, ny)
                lanes = pl.ds(x * LANES, LANES)
                root_t = jnp.sqrt(heat[span].reshape(shape3))
                total = jnp.zeros(shape3, F32)
                volume = jnp.zeros(shape3, F32)
                for i in range(nc):
                    o = amount_v[i, span].reshape(shape3)
                    v = jnp.abs(table_v[0, i] - table_v[1, i] * root_t) * o
                    total += o
                    volume += table_v[2, i] * o
                    high, low = pieces_of(v.reshape(ny, LANES), 2)
                    split_v[pl.ds(i * ny, ny), lanes] = high
                    split_v[pl.ds(size + i * ny, ny), lanes] = low
                    split_v[pl.ds(2 * size + i * ny, ny), lanes] = high
                field_v[0, span] = total.reshape(ny, LANES)
                field_v[1, span] = volume.reshape(ny, LANES)
            lanes = pl.ds(c * per * LANES, per * LANES)
            mixed = mat(mixer, split_v[:, lanes])
            for k in range(per):
                x = c * per + k
                span = pl.ds(x * ny, ny)
                root_t = jnp.sqrt(heat[span].reshape(shape3))
                total = jnp.zeros(shape3, F32)
                for i in range(nc):
                    m = mixed[i * ny : (i + 1) * ny, k * LANES : (k + 1) * LANES].reshape(shape3)
                    psi = jnp.abs(table_v[0, i] - table_v[1, i] * root_t) * m
                    total += amount_v[i, span].reshape(shape3) * psi
                    psi_v[i, span] = psi.reshape(ny, LANES)
                field_v[2, span] = total.reshape(ny, LANES)

        span = pl.ds(h * half * rows, half * rows)
        p, t = press[span], heat[span]
        liquid = flag[span] == 1
        r = 1.0 / field_v[0, span]
        rt = 1.0 / t
        ratio_pt = p * rt
        g = ratio_pt * rt
        beta = field_v[1, span] * r
        gr = g * r
        big_a = gr * r * field_v[2, span]
        big_b = ratio_pt * beta
        z = jnp.where(liquid, big_b + 0.01, 1.0 + big_b)
        floor = big_b + 0.01
        c2 = big_b - 1.0
        c1 = big_a - 3.0 * big_b * big_b - 2.0 * big_b
        c0 = big_b * big_b + big_b * big_b * big_b - big_a * big_b
        twice = 2.0 * c2
        for _ in range(NEWT):
            value = ((z + c2) * z + c1) * z + c0
            incline = (3.0 * z + twice) * z + c1
            z = jnp.maximum(z - value / jnp.maximum(incline, 0.1), floor)
        log_ratio = jnp.log((z + (1.0 + ROOT_TWO) * big_b) / (z + (1.0 - ROOT_TWO) * big_b))
        lb = log_ratio / (ROOT_TWO * big_b)
        e0 = jnp.log(z - big_b)
        e1 = (z - 1.0 + 0.5 * big_a * lb) / beta
        e2 = gr * lb
        rho = ratio_pt / z
        mob = rho / jnp.where(liquid, visc[1], visc[0])
        mob_out[span] = mob
        field_v[0, span] = e0
        field_v[1, span] = e1
        field_v[2, span] = e2
        field_v[3, span] = mob * r
        for x in range(h * half * per, (h + 1) * half * per):
            span = pl.ds(x * ny, ny)
            e0, e1, e2, mr = (field_v[k, span].reshape(shape3) for k in range(4))
            for i in range(nc):
                value = table_v[2, i] * e1 - e0 - psi_v[i, span].reshape(shape3) * e2
                lnphi_v[i, span] = value.reshape(ny, LANES).astype(BF16)
                carried_v[i, span] = (mr * amount_v[i, span].reshape(shape3)).reshape(ny, LANES)
        span = pl.ds(h * half * rows, half * rows)
        for source, target in ((lnphi_v, lnphi_out), (carried_v, carried_out)):
            copy = pltpu.make_async_copy(
                source.at[:, span], target.at[:, span], out_sems.at[len(stores)]
            )
            copy.start()
            stores.append(copy)

    odd_g = lax.axis_index(axes[0]) % 2 == 1
    odd_s = lax.axis_index(axes[1]) % 2 == 1
    many = edge_x_out.shape[0]
    for k in range(many):
        at_low = odd_g if k == 0 else jnp.logical_not(odd_g)
        span = pl.ds(pl.multiple_of(jnp.where(at_low, 0, (nx - 1) * ny), ny), ny)
        for source, target in (
            (carried_v.at[:, span], edge_x_out.at[k, pl.ds(0, nc)]),
            (press.at[span], edge_x_out.at[k, nc]),
            (perm.at[span], edge_x_out.at[k, nc + 1]),
        ):
            copy = pltpu.make_async_copy(source, target, edge_sem.at[0])
            copy.start()
            stores.append(copy)
    low, high = pl.ds(0, nx, stride=ny), pl.ds(ny - 1, nx, stride=ny)
    for i in range(nc + 2):
        if i < nc:
            a, b = carried_v[i, low], carried_v[i, high]
        else:
            source = press if i == nc else perm
            a, b = source[low], source[high]
        edge_ya_out[i] = jnp.where(odd_s, a, b)
        edge_yb_out[i] = jnp.where(odd_s, b, a)

    row_hot, lane_hot = place_hots(loc[...], nx * ny)
    lane_hot = hot(lane_hot)

    def cells_of(field):
        return jnp.sum(jnp.where(row_hot, mat_hot(field, lane_hot), 0.0), axis=0, keepdims=True)

    p_cell = cells_of(press[...])
    pcell_out[...] = p_cell
    weight = strength[...] * cells_of(mob_out[...])
    segments = part_out.shape[1] // 2
    seg_hot = iota((segments, loc.shape[1]), 0) == seg[...]
    sums = jnp.concatenate(
        [jnp.where(seg_hot, weight, 0.0), jnp.where(seg_hot, weight * (p_cell - 1.0), 0.0)], axis=0
    )
    slot_hot = slot_hot_of(member[...], place[...])
    part_out[...] = hot_mat_nt(slot_hot.astype(BF16), sums)
    for copy in stores:
        copy.wait()


def flux_kernel(
    nx,
    ny,
    axes,
    carried,
    press,
    perm,
    pore,
    flag,
    mob,
    old,
    edge_x,
    edge_ya,
    edge_yb,
    parts,
    seg_press,
    loc,
    member,
    seg,
    strength,
    place,
    pcell,
    trans,
    visc,
    inject,
    own_press,
    order,
    exit_press,
    friction,
    resid_out,
    well_out,
    c_v,
    p_v,
    k_v,
    y_v,
    old_v,
    res_v,
    in_sems,
    out_sems,
):
    nc = carried.shape[0]
    step = ny + 2 * MARGIN
    g, s = lax.axis_index(axes[0]), lax.axis_index(axes[1])
    ng, ns = lax.axis_size(axes[0]), lax.axis_size(axes[1])
    odd_g, odd_s = g % 2, s % 2
    has_low_y, has_high_y = s > 0, s < ns - 1
    has_low_x, has_high_x = g > 0, g < ng - 1

    def inner(x):
        return pl.ds((x + 1) * step + MARGIN, ny)

    copies = []

    def go(source, target, sem):
        copy = pltpu.make_async_copy(source, target, sem)
        copy.start()
        return copy

    edge_copies = [
        go(edge_ya.at[1 - odd_s], y_v.at[1 - odd_s], in_sems.at[0]),
        go(edge_yb.at[odd_s], y_v.at[odd_s], in_sems.at[0]),
    ]
    for k in range(edge_x.shape[0]):
        mine = 1 - odd_g if k == 0 else odd_g
        plane = jnp.where(mine == 1, nx + 1, 0)
        span = pl.ds(pl.multiple_of(plane * step + MARGIN, MARGIN), ny)
        edge_copies.append(go(edge_x.at[k, mine, pl.ds(0, nc)], c_v.at[:, span], in_sems.at[0]))
        edge_copies.append(go(edge_x.at[k, mine, nc], p_v.at[span], in_sems.at[0]))
        edge_copies.append(go(edge_x.at[k, mine, nc + 1], k_v.at[span], in_sems.at[0]))
    plane_copies = []
    for x in range(nx):
        span = pl.ds(x * ny, ny)
        plane_copies.append(
            [
                go(carried.at[:, span], c_v.at[:, inner(x)], in_sems.at[1 + x]),
                go(old.at[:, span], old_v.at[:, span], in_sems.at[1 + x]),
            ]
        )
    for x in range(nx):
        span = pl.ds(x * ny, ny)
        p_v[inner(x)] = press[span]
        k_v[inner(x)] = perm[span]
    if edge_x.shape[0] == 1:
        plane = jnp.where(odd_g == 1, nx + 1, 0)
        span = pl.ds(pl.multiple_of(plane * step + MARGIN, MARGIN), ny)
        zero = jnp.zeros((ny, LANES), F32)
        p_v[span] = zero
        k_v[span] = zero
        for i in range(nc):
            c_v[i, span] = zero

    row_hot, lane_hot = place_hots(loc[...], nx * ny)
    slot_hot = slot_hot_of(member[...], place[...])
    segments = own_press.shape[1]
    seg_hot = hot(iota((segments, loc.shape[1]), 0) == seg[...])
    p_seg = jnp.sum(mat_hot(seg_press[...], seg_hot) * slot_hot, axis=0, keepdims=True)
    push = strength[...] * (pcell[...] - p_seg)
    flows = jnp.concatenate(
        [
            jnp.where(lane_hot, jnp.maximum(push, 0.0), 0.0),
            jnp.where(lane_hot, jnp.minimum(push, 0.0), 0.0),
        ],
        axis=0,
    )
    spread = hot_mat_nt(hot(row_hot), flows, 2)

    gathered = jnp.sum(parts[...], axis=0)
    own = jnp.sum(jnp.where(iota(gathered.shape, 0) == s, gathered, 0.0), axis=0, keepdims=True)
    well_p = own_press[...]
    rate = own[:, segments:] - (well_p - 1.0) * own[:, :segments]
    order_hot = hot(iota((segments, segments), 0) == order[...])
    both = mat_hot(jnp.concatenate([rate, well_p], axis=0), order_hot)
    upper = hot(iota((segments, segments), 0) <= iota((segments, segments), 1))
    running = mat_hot(both[0:1], upper)
    press_ord = both[1:2]
    after = hot(iota((segments, segments), 0) == iota((segments, segments), 1) + 1)
    last = iota((1, segments), 1) == segments - 1
    nexts = jnp.where(last, exit_press[0], mat_hot(press_ord, after))
    res_ord = press_ord - nexts - friction[0] * running * jnp.abs(running)
    well_out[...] = sum(mat_nt(piece, order_hot) for piece in pieces_of(res_ord, 3))

    for copy in edge_copies:
        copy.wait()
    for side in range(2):
        start = step + (MARGIN - 1 if side == 0 else MARGIN + ny)
        span = pl.ds(start, nx, stride=step)
        for i in range(nc):
            c_v[i, span] = y_v[side, i]
        p_v[span] = y_v[side, nc]
        k_v[span] = jnp.where(has_low_y if side == 0 else has_high_y, y_v[side, nc + 1], 0.0)

    lane = iota((ny, LANES), 1)
    share = 1.0 / sum(jnp.full((ny, LANES), inject[i], F32) for i in range(nc))
    stores = []
    for x in range(nx):
        base = (x + 1) * step + MARGIN
        here = pl.ds(base, ny)
        rows = pl.ds(x * ny, ny)
        p_a, k_a = p_v[here], k_v[here]

        def face(p_b, k_b, axis):
            t = 2.0 * trans[axis] * k_a * k_b / (k_a + k_b)
            flow = t * (p_a - p_b)
            return jnp.maximum(flow, 0.0), jnp.minimum(flow, 0.0)

        spots = [
            (pl.ds(base + step, ny), 0),
            (pl.ds(base - step, ny), 0),
            (pl.ds(base + 1, ny), 1),
            (pl.ds(base - 1, ny), 1),
        ]
        centre = pore[rows] * jnp.where(flag[rows] == 1, visc[1], visc[0])
        centre += spread[x * ny : (x + 1) * ny, :LANES]
        ins = []
        for k, (spot, axis) in enumerate(spots):
            k_b = k_v[spot]
            if k == 0 and x == nx - 1:
                k_b = jnp.where(has_high_x, k_b, 0.0)
            if k == 1 and x == 0:
                k_b = jnp.where(has_low_x, k_b, 0.0)
            out, into = face(p_v[spot], k_b, axis)
            centre += out
            ins.append(into)
        for shift, edge in ((LANES - 1, LANES - 1), (1, 0)):
            k_b = jnp.where(lane == edge, 0.0, pltpu.roll(k_a, shift, 1))
            out, into = face(pltpu.roll(p_a, shift, 1), k_b, 2)
            centre += out
            ins.append(into)
        pushed = mob[rows] * spread[x * ny : (x + 1) * ny, LANES:] * share
        for copy in plane_copies[x]:
            copy.wait()
        if x + 1 < nx:
            for copy in plane_copies[x + 1]:
                copy.wait()
            plane_copies[x + 1] = []
        for i in range(nc):
            c = c_v[i, here]
            value = centre * c - old_v[i, rows] + inject[i] * pushed
            for into, (spot, _) in zip(ins[:4], spots):
                value += into * c_v[i, spot]
            value += ins[4] * pltpu.roll(c, LANES - 1, 1)
            value += ins[5] * pltpu.roll(c, 1, 1)
            res_v[i, rows] = value
        stores.append(go(res_v.at[:, rows], resid_out.at[:, rows], out_sems.at[x]))
    for copy in stores:
        copy.wait()


def pairs_of(count, other):
    return [[i, (i + 1) % count] for i in range(1 if other else 0, count, 2)]


def per_device(
    amount,
    press,
    heat,
    flag,
    perm,
    pore,
    old,
    trans,
    visc,
    crit,
    attract,
    covol,
    slope,
    coupling,
    inject,
    locale,
    member,
    seg,
    strength,
    place,
    order,
    seg_press,
    exit_press,
    friction,
):
    axes = ("grp", "sub")
    nc, nx, ny, nz = amount.shape
    ng, ns = lax.axis_size("grp"), lax.axis_size("sub")
    rows = nx * ny
    perfs = locale.shape[0]
    wells, segments = place.shape[1], seg_press.shape[1]
    flat = lambda a: a.reshape(a.shape[:-3] + (rows, nz))
    line = lambda a: a.reshape(1, perfs)
    vm = pl.BlockSpec(memory_space=pltpu.VMEM)
    sm = pl.BlockSpec(memory_space=pltpu.SMEM)
    hbm = pl.BlockSpec(memory_space=pl.ANY)
    many_x = 1 if ng == 2 else 2

    amount, old = flat(amount), flat(old)
    press, heat, flag, perm, pore = (flat(a) for a in (press, heat, flag, perm, pore))
    locale, member, seg, strength = (line(a) for a in (locale, member, seg, strength))

    all_press = lax.all_gather(seg_press, "sub", tiled=True)

    lnphi, carried, mob, edge_x, edge_ya, edge_yb, part, pcell = pl.pallas_call(
        functools.partial(phase_kernel, nx, ny, axes),
        out_shape=(
            jax.ShapeDtypeStruct((nc, rows, nz), BF16),
            jax.ShapeDtypeStruct((nc, rows, nz), F32),
            jax.ShapeDtypeStruct((rows, nz), F32),
            jax.ShapeDtypeStruct((many_x, nc + 2, ny, nz), F32),
            jax.ShapeDtypeStruct((nc + 2, nx, nz), F32),
            jax.ShapeDtypeStruct((nc + 2, nx, nz), F32),
            jax.ShapeDtypeStruct((wells, 2 * segments), F32),
            jax.ShapeDtypeStruct((1, perfs), F32),
        ),
        in_specs=[hbm] + [vm] * 4 + [sm] * 5 + [vm] * 6,
        out_specs=(hbm, hbm, vm, hbm, vm, vm, vm, vm),
        scratch_shapes=[
            pltpu.VMEM((nc, rows, nz), F32),
            pltpu.VMEM((3 * nc * ny, nx * nz), BF16),
            pltpu.VMEM((nc, rows, nz), F32),
            pltpu.VMEM((nc, rows, nz), F32),
            pltpu.VMEM((nc, rows, nz), BF16),
            pltpu.VMEM((4, rows, nz), F32),
            pltpu.VMEM((3, nc, SUBLANES, LANES), F32),
            pltpu.SemaphoreType.DMA((nx // 2,)),
            pltpu.SemaphoreType.DMA((4,)),
            pltpu.SemaphoreType.DMA((1,)),
        ],
        compiler_params=pltpu.CompilerParams(vmem_limit_bytes=VMEM_LIMIT),
        name="phase",
    )(
        amount, press, heat, flag, perm, visc, crit, attract, covol, slope, coupling,
        locale, member, seg, strength, place,
    )

    groups_a, groups_b = pairs_of(ns, False), pairs_of(ns, True)
    got_ya = lax.all_gather(edge_ya, "sub", axis_index_groups=groups_a)
    got_yb = lax.all_gather(edge_yb, "sub", axis_index_groups=groups_b)
    got_x = [
        lax.all_gather(edge_x[k], "grp", axis_index_groups=pairs_of(ng, k == 1))
        for k in range(many_x)
    ]
    got_x = got_x[0][None] if many_x == 1 else jnp.stack(got_x)
    parts = lax.all_gather(part, "sub")

    resid, well = pl.pallas_call(
        functools.partial(flux_kernel, nx, ny, axes),
        out_shape=(
            jax.ShapeDtypeStruct((nc, rows, nz), F32),
            jax.ShapeDtypeStruct((1, segments), F32),
        ),
        in_specs=[hbm] + [vm] * 5 + [hbm] * 4 + [vm] * 8 + [sm] * 3 + [vm] * 2 + [sm] * 2,
        out_specs=(hbm, vm),
        scratch_shapes=[
            pltpu.VMEM((nc, (nx + 2) * (ny + 2 * MARGIN), nz), F32),
            pltpu.VMEM(((nx + 2) * (ny + 2 * MARGIN), nz), F32),
            pltpu.VMEM(((nx + 2) * (ny + 2 * MARGIN), nz), F32),
            pltpu.VMEM((2, nc + 2, nx, nz), F32),
            pltpu.VMEM((nc, rows, nz), F32),
            pltpu.VMEM((nc, rows, nz), F32),
            pltpu.SemaphoreType.DMA((1 + nx,)),
            pltpu.SemaphoreType.DMA((nx,)),
        ],
        compiler_params=pltpu.CompilerParams(vmem_limit_bytes=VMEM_LIMIT),
        name="flux",
    )(
        carried, press, perm, pore, flag, mob, old, got_x, got_ya, got_yb, parts, all_press,
        locale, member, seg, strength, place, pcell,
        trans, visc, inject, seg_press, order, exit_press, friction,
    )
    block = (nc, nx, ny, nz)
    return resid.reshape(block), lnphi.reshape(block), well


def solution(mesh):
    cells, parts = P("grp", "sub", None), P(None, "grp", "sub", None)
    listed = P(("grp", "sub"))
    row = P(("grp", "sub"), None)
    in_specs = (
        (parts,) + (cells,) * 5 + (parts,) + (P(),) * 8
        + (listed, row, listed, listed, P("grp", None), row, row, listed, listed)
    )
    return jax.shard_map(
        per_device, mesh=mesh, in_specs=in_specs, out_specs=(parts, parts, row), check_vma=False
    )
```

time: 111 us -> 73.8 us (0.66)
  the two profiles are of different devices: /device:TPU:10 before, /device:TPU:0 now
where the time goes in v1:
time: 73.8 us; the launch traced here: 73.3 us
  blocking collectives  55.9 us (76%)
  Pallas kernels  8.87 us (12%)
  local copies, waits for them, and re-layouts  6.53 us (9%)
  between operations  2.08 us (3%)
    all_gather x1, blocking collectives, per_device(): all_press = lax.all_gather(seg_press, 'sub', tiled=True)  23.1 us
    all_gather x1, blocking collectives, per_device(): parts = lax.all_gather(part, 'sub')  17.7 us
    all_gather x1, blocking collectives, per_device(): got_yb = lax.all_gather(edge_yb, 'sub', axis_index_groups=groups_b)  7.14 us
    unnamed x46, local copies, waits for them, and re-layouts  6.53 us
    all_gather x1, blocking collectives, per_device(): lax.all_gather(edge_x[k], 'grp', axis_index_groups=pairs_of(ng, k == 1))  5.94 us
    pallas_call x1, Pallas kernels, per_device(): pl.pallas_call(functools.partial(flux_kernel, nx, ny, axes), out_shape=(j...  4.44 us
    pallas_call x1, Pallas kernels, per_device(): pl.pallas_call(functools.partial(phase_kernel, nx, ny, axes), out_shape=(...  4.43 us
    all_gather x1, blocking collectives, per_device(): got_ya = lax.all_gather(edge_ya, 'sub', axis_index_groups=groups_a)  1.9 us

profile of v1, /device:TPU:0, one launch (start us, length us, event | category | flops | bytes accessed | tf_op | source)
XLA Modules:
  0.0 73.3 jit_solution(16883136248216704325)
XLA Ops:
  1.9 0.0 copy-start.15
  1.9 0.0 copy-start.8
  1.9 0.6 copy-done.15
  2.6 0.0 copy-start.10
  2.6 0.0 copy-start.11
  2.6 0.0 copy-start.12
  2.6 0.0 copy-start.16
  2.6 0.0 copy-start.17
  2.6 0.0 copy-start.18
  2.6 0.0 copy-start.19
  2.6 23.1 %all-gather.3 = f32[16,1,32]{2,1,0:T(1,128)S(1)} all-gather(f32[1,1,32]{2,1,0:T(1,128)S(1)} %bitcast.42), channel_id=1, replica_groups=mesh['grp'=2,'sub'=16] {'sub'}, dimensions={0}, use_global_device_ids=true | all-gather | bytes 2176 | tf_op jit(solution)/shard_map/all_gather | solution.py:499
  25.8 0.0 copy-start.9
  25.8 0.0 copy-start.13
  25.8 0.0 copy-done.8
  25.8 0.0 copy-done.10
  25.8 0.0 copy-done.11
  25.8 0.0 copy-done.12
  25.8 0.0 copy-done.14
  25.8 0.0 copy-done.16
  25.8 0.0 copy-done.17
  25.8 0.0 copy-done.18
  25.8 0.0 copy-done.19
  25.8 0.6 copy-done.9
  26.4 0.0 copy-done.13
  26.4 0.0 copy-start
  26.4 1.2 %copy-done = f32[16,8,16,128]{3,2,1,0:T(8,128)S(1)} copy-done((f32[16,8,16,128]{3,2,1,0:T(8,128)S(1)}, f32[16,8,16,128]{3,2,1,0:T(8,128)}, u32[]{:S(2)}) %copy-start) | copy-done | bytes 1048600
  27.7 0.0 copy-start.2
  27.7 0.8 %copy-done.2 = f32[8,16,128]{2,1,0:T(8,128)S(1)} copy-done((f32[8,16,128]{2,1,0:T(8,128)S(1)}, f32[8,16,128]{2,1,0:T(8,128)}, u32[]{:S(2)}) %copy-start.2) | copy-done | bytes 65560
  28.5 0.0 copy-start.3
  28.5 0.8 %copy-done.3 = s32[8,16,128]{2,1,0:T(8,128)S(1)} copy-done((s32[8,16,128]{2,1,0:T(8,128)S(1)}, s32[8,16,128]{2,1,0:T(8,128)}, u32[]{:S(2)}) %copy-start.3) | copy-done | bytes 65560
  29.4 0.0 copy-start.4
  29.4 0.8 %copy-done.4 = f32[8,16,128]{2,1,0:T(8,128)S(1)} copy-done((f32[8,16,128]{2,1,0:T(8,128)S(1)}, f32[8,16,128]{2,1,0:T(8,128)}, u32[]{:S(2)}) %copy-start.4) | copy-done | bytes 65560
  30.2 0.0 copy-start.6
  30.2 0.8 %copy-done.6 = f32[8,16,128]{2,1,0:T(8,128)S(1)} copy-done((f32[8,16,128]{2,1,0:T(8,128)S(1)}, f32[8,16,128]{2,1,0:T(8,128)}, u32[]{:S(2)}) %copy-start.6) | copy-done | bytes 65560
  31.0 0.0 copy-start.1
  31.0 4.4 %phase.1 = (bf16[16,128,128]{2,1,0:T(8,128)(2,1)}, f32[16,128,128]{2,1,0:T(8,128)S(1)}, f32[128,128]{1,0:T(8,128)S(1)}, f32[1,18,16,128]{3,2,1,0:T(8,128)S(1)}, ...) custom-call(f32[16,128,128]{2,1,0:T(8,128)S(1)} %bitcast.20, ...), custom_call_target="tpu_custom_call" | custom-call | tf_op jit(solution)/shard_map/phase/pallas_call | solution.py:501
  35.5 17.7 %all-gather.2 = f32[256,64]{1,0:T(8,128)S(1)} all-gather(f32[16,64]{1,0:T(8,128)S(1)} %get-tuple-element.18), channel_id=4, replica_groups=mesh['grp'=2,'sub'=16] {'sub'}, dimensions={0}, use_global_device_ids=true | all-gather | bytes 69632 | tf_op jit(solution)/shard_map/all_gather | solution.py:542
  53.2 1.9 %all-gather = f32[36,8,128]{2,1,0:T(8,128)S(1)} all-gather(f32[18,8,128]{2,1,0:T(8,128)S(1)} %get-tuple-element.16), channel_id=2, replica_groups={{0,1},{2,3},{4,5},{6,7},{8,9},{10,11},{12,13},{14,15},{16,17},{18,19},{..., dimensions={0}, use_global_device_ids=true | all-gather | bytes 221184 | tf_op jit(solution)/shard_map/all_gather | solution.py:535
  55.1 7.1 %all-gather.1 = f32[36,8,128]{2,1,0:T(8,128)S(1)} all-gather(f32[18,8,128]{2,1,0:T(8,128)S(1)} %get-tuple-element.17), channel_id=3, replica_groups={{1,2},{3,4},{5,6},{7,8},{9,10},{11,12},{13,14},{15,0},{17,18},{19,20},{..., dimensions={0}, use_global_device_ids=true | all-gather | bytes 221184 | tf_op jit(solution)/shard_map/all_gather | solution.py:536
  62.3 0.0 copy-start.5
  62.3 5.9 %all_gather.24 = f32[2,18,16,128]{3,2,1,0:T(8,128)S(1)} all-gather(f32[1,18,16,128]{3,2,1,0:T(8,128)S(1)} %get-tuple-element.15), channel_id=1, replica_groups={{0,16},{1,17},{2,18},{3,19},{4,20},{5,21},{6,22},{7,23},{8,24},{9,25},{..., dimensions={0}, use_global_device_ids=true | all-gather | bytes 442368 | tf_op jit(solution)/shard_map/all_gather | solution.py:538
  68.2 0.0 copy-done.1
  68.2 0.0 copy-done.5
  68.2 0.0 copy-done.7
  68.2 0.6 copy-done.20
  68.9 0.0 copy-done.21
  68.9 0.0 copy-done.22
  68.9 4.4 %flux.1 = (f32[16,128,128]{2,1,0:T(8,128)}, f32[1,32]{1,0:T(1,128)}) custom-call(f32[16,128,128]{2,1,0:T(8,128)S(1)} %get-tuple-element.13.carried, f32[128,128]{1,0:T(8,128)S(1)} %bitcast.26, f32[128,128]{1,0:T(8,128)S(1)} %bitcast.30, f32[128,128]{1,0:T(8,128)S(1)} %bitcast.32, s32[128,128]{1,0:T(8,128)S(1)} %bitcast.28, ...), custom_call_target="tpu_custom_call" | custom-call | tf_op jit(solution)/shard_map/flux/pallas_call | solution.py:544
  (5 shorter events, 0.0 us)
Async XLA Ops:
  1.9 0.7 copy-start.15
  1.9 23.8 %copy-start.8 = (f32[16,16]{1,0:T(8,128)S(1)}, f32[16,16]{1,0:T(8,128)}, u32[]{:S(2)}) copy-start(f32[16,16]{1,0:T(8,128)} %coupling.1) | copy-start | bytes 3076
  2.6 23.2 %copy-start.10 = (s32[256,1]{0,1:T(1,128)S(1)}, s32[256,1]{0,1:T(1,128)}, u32[]{:S(2)}) copy-start(s32[256,1]{0,1:T(1,128)} %param.40) | copy-start | bytes 3076
  2.6 23.2 %copy-start.11 = (s32[256]{0:T(256)S(1)}, s32[256]{0:T(256)}, u32[]{:S(2)}) copy-start(s32[256]{0:T(256)} %param.41) | copy-start | bytes 3076
  2.6 23.2 %copy-start.12 = (f32[256]{0:T(256)S(1)}, f32[256]{0:T(256)}, u32[]{:S(2)}) copy-start(f32[256]{0:T(256)} %param.42) | copy-start | bytes 3076
  2.6 23.2 %copy-start.14 = (s32[1,16]{1,0:T(1,128)S(1)}, s32[1,16]{1,0:T(1,128)}, u32[]{:S(2)}) copy-start(s32[1,16]{1,0:T(1,128)} %place.3) | copy-start | bytes 196
  2.6 23.2 %copy-start.16 = (f32[16]{0:T(128)S(1)}, f32[16]{0:T(128)}, u32[]{:S(2)}) copy-start(f32[16]{0:T(128)} %crit.1) | copy-start | bytes 196
  2.6 23.2 %copy-start.17 = (f32[16]{0:T(128)S(1)}, f32[16]{0:T(128)}, u32[]{:S(2)}) copy-start(f32[16]{0:T(128)} %attract.1) | copy-start | bytes 196
  2.6 23.2 %copy-start.18 = (f32[16]{0:T(128)S(1)}, f32[16]{0:T(128)}, u32[]{:S(2)}) copy-start(f32[16]{0:T(128)} %covol.1) | copy-start | bytes 196
  2.6 23.2 %copy-start.19 = (f32[16]{0:T(128)S(1)}, f32[16]{0:T(128)}, u32[]{:S(2)}) copy-start(f32[16]{0:T(128)} %slope.1) | copy-start | bytes 196
  25.8 0.7 copy-start.9
  25.8 0.7 copy-start.13
  26.4 1.2 %copy-start = (f32[16,8,16,128]{3,2,1,0:T(8,128)S(1)}, f32[16,8,16,128]{3,2,1,0:T(8,128)}, u32[]{:S(2)}) copy-start(f32[16,8,16,128]{3,2,1,0:T(8,128)} %param.24) | copy-start | bytes 3145732
  27.7 0.8 %copy-start.2 = (f32[8,16,128]{2,1,0:T(8,128)S(1)}, f32[8,16,128]{2,1,0:T(8,128)}, u32[]{:S(2)}) copy-start(f32[8,16,128]{2,1,0:T(8,128)} %param.25) | copy-start | bytes 196612
  28.5 0.8 %copy-start.3 = (s32[8,16,128]{2,1,0:T(8,128)S(1)}, s32[8,16,128]{2,1,0:T(8,128)}, u32[]{:S(2)}) copy-start(s32[8,16,128]{2,1,0:T(8,128)} %param.27) | copy-start | bytes 196612
  29.4 0.8 %copy-start.4 = (f32[8,16,128]{2,1,0:T(8,128)S(1)}, f32[8,16,128]{2,1,0:T(8,128)}, u32[]{:S(2)}) copy-start(f32[8,16,128]{2,1,0:T(8,128)} %param.28) | copy-start | bytes 196612
  30.2 0.8 %copy-start.6 = (f32[8,16,128]{2,1,0:T(8,128)S(1)}, f32[8,16,128]{2,1,0:T(8,128)}, u32[]{:S(2)}) copy-start(f32[8,16,128]{2,1,0:T(8,128)} %param.26) | copy-start | bytes 196612
  31.0 37.2 %copy-start.1 = (f32[16,8,16,128]{3,2,1,0:T(8,128)S(1)}, f32[16,8,16,128]{3,2,1,0:T(8,128)}, u32[]{:S(2)}) copy-start(f32[16,8,16,128]{3,2,1,0:T(8,128)} %param.30) | copy-start | bytes 3145732
  62.3 6.0 %copy-start.5 = (f32[8,16,128]{2,1,0:T(8,128)S(1)}, f32[8,16,128]{2,1,0:T(8,128)}, u32[]{:S(2)}) copy-start(f32[8,16,128]{2,1,0:T(8,128)} %param.28) | copy-start | bytes 196612
  62.3 6.0 %copy-start.7 = (f32[8,16,128]{2,1,0:T(8,128)S(1)}, f32[8,16,128]{2,1,0:T(8,128)}, u32[]{:S(2)}) copy-start(f32[8,16,128]{2,1,0:T(8,128)} %param.29) | copy-start | bytes 196612
  68.2 0.7 copy-start.20
  68.2 0.7 copy-start.21
  68.2 0.7 copy-start.22

commit v2 on v1

v2 whole, which is shorter than its diff:
```python
import functools
import math

import jax
import jax.numpy as jnp
from jax import lax
from jax.experimental import pallas as pl
from jax.experimental.pallas import tpu as pltpu
from jax.sharding import PartitionSpec as P

NEWT = 8
ROOT_TWO = math.sqrt(2.0)
LANES = 128
SUBLANES = 8
F32 = jnp.float32
BF16 = jnp.bfloat16
VMEM_LIMIT = 48 * 1024 * 1024
MARGIN = 8
SMALL, FIELDS = 14, 4


def iota(shape, dim):
    return lax.broadcasted_iota(jnp.int32, shape, dim)


def pieces_of(x, count):
    out = []
    for _ in range(count):
        piece = x.astype(BF16)
        out.append(piece)
        x = x - piece.astype(F32)
    return out


def mat(a, b):
    return lax.dot_general(a, b, (((1,), (0,)), ((), ())), preferred_element_type=F32)


def mat_nt(a, b):
    return lax.dot_general(a, b, (((1,), (1,)), ((), ())), preferred_element_type=F32)


def mat_hot(x, hot, count=3):
    return sum(mat(piece, hot) for piece in pieces_of(x, count))


def hot_mat_nt(hot, x, count=3):
    return sum(mat_nt(hot, piece) for piece in pieces_of(x, count))


def inverse(x):
    r = pl.reciprocal(x, approx=True)
    return r * (2.0 - x * r)


def hot(cond):
    return jnp.where(cond, 1.0, 0.0).astype(BF16)


def place_hots(loc, rows):
    n = loc.shape[1]
    row_hot = iota((rows, n), 0) == loc // LANES
    lane_hot = iota((LANES, n), 0) == loc % LANES
    return row_hot, lane_hot


def slot_hot_of(member, place):
    wells = place.shape[1]
    slot_of = hot(iota((wells, wells), 0) == place)
    member_hot = hot(iota((wells, member.shape[1]), 0) == member)
    return mat(slot_of, member_hot)


def phase_kernel(
    nx,
    ny,
    axes,
    amount,
    *rest,
):
    count = SMALL + FIELDS
    sources, rest = rest[:count], rest[count:]
    (
        lnphi_out,
        carried_out,
        mob_out,
        edge_x_out,
        edge_ya_out,
        edge_yb_out,
        part_out,
        pcell_out,
        consts_out,
    ) = rest[:9]
    targets, rest = rest[9 : 9 + count], rest[9 + count :]
    amount_v, split_v, psi_v, lnphi_v, field_v, table_v, small_sems, in_sems, out_sems = rest
    visc, crit, attract, covol, slope, trans, inject = targets[:7]
    coupling, loc, member, seg, strength, place, own_press = targets[7 : SMALL]
    heat, press, flag, perm = targets[SMALL :]
    nc = amount.shape[0]
    per = 2
    chunks = nx // per
    rows = per * ny

    def go(source, target, sem):
        copy = pltpu.make_async_copy(source, target, sem)
        copy.start()
        return copy

    small = [go(a, b, small_sems.at[k]) for k, (a, b) in enumerate(zip(sources, targets))]
    heat_load, press_load, flag_load, perm_load = small[SMALL :]
    loads = []
    for c in range(chunks):
        span = pl.ds(c * rows, rows)
        loads.append(go(amount.at[:, span], amount_v.at[:, span], in_sems.at[c]))
    for copy in small[: SMALL]:
        copy.wait()

    for i in range(nc):
        root = jnp.sqrt(jnp.full((SUBLANES, LANES), attract[i], F32))
        kappa = jnp.full((SUBLANES, LANES), slope[i], F32)
        tc = jnp.full((SUBLANES, LANES), crit[i], F32)
        table_v[0, i] = root * (1.0 + kappa)
        table_v[1, i] = root * kappa / jnp.sqrt(tc)
        table_v[2, i] = jnp.full((SUBLANES, LANES), covol[i], F32)

    total = sum(inject[i] for i in range(nc))
    share = 1.0 / jnp.full((SUBLANES, LANES), total, F32)
    numbers = [trans[0], trans[1], trans[2], visc[0], visc[1]]
    for i in range(nc):
        consts_out[i] = inject[i] * share
    for i, number in enumerate(numbers):
        consts_out[nc + i] = jnp.full((SUBLANES, LANES), number, F32)

    size = nc * ny
    spread = hot(iota((size, nc), 0) // ny == iota((size, nc), 1))
    same_row = iota((size, size), 0) % ny == iota((size, size), 1) % ny
    mixers = []
    for piece in pieces_of(1.0 - coupling[...], 2):
        wide = mat(spread, piece).astype(BF16)
        mixers.append(jnp.where(same_row, mat_nt(wide, spread), 0.0).astype(BF16))
    mixer = jnp.concatenate([mixers[0], mixers[0], mixers[1]], axis=1)

    shape3 = (ny // SUBLANES, SUBLANES, LANES)
    stores = []
    half = chunks // 2
    heat_load.wait()
    for h in range(2):
        for c in range(h * half, (h + 1) * half):
            loads[c].wait()
            for x in range(c * per, (c + 1) * per):
                span = pl.ds(x * ny, ny)
                lanes = pl.ds(x * LANES, LANES)
                root_t = jnp.sqrt(heat[span].reshape(shape3))
                total = jnp.zeros(shape3, F32)
                volume = jnp.zeros(shape3, F32)
                for i in range(nc):
                    o = amount_v[i, span].reshape(shape3)
                    v = jnp.abs(table_v[0, i] - table_v[1, i] * root_t) * o
                    total += o
                    volume += table_v[2, i] * o
                    high, low = pieces_of(v.reshape(ny, LANES), 2)
                    split_v[pl.ds(i * ny, ny), lanes] = high
                    split_v[pl.ds(size + i * ny, ny), lanes] = low
                    split_v[pl.ds(2 * size + i * ny, ny), lanes] = high
                field_v[0, span] = total.reshape(ny, LANES)
                field_v[1, span] = volume.reshape(ny, LANES)
            lanes = pl.ds(c * per * LANES, per * LANES)
            mixed = mat(mixer, split_v[:, lanes])
            for k in range(per):
                x = c * per + k
                span = pl.ds(x * ny, ny)
                root_t = jnp.sqrt(heat[span].reshape(shape3))
                total = jnp.zeros(shape3, F32)
                for i in range(nc):
                    m = mixed[i * ny : (i + 1) * ny, k * LANES : (k + 1) * LANES].reshape(shape3)
                    psi = jnp.abs(table_v[0, i] - table_v[1, i] * root_t) * m
                    total += amount_v[i, span].reshape(shape3) * psi
                    psi_v[i, span] = psi.reshape(ny, LANES)
                field_v[2, span] = total.reshape(ny, LANES)

        if h == 0:
            press_load.wait()
            flag_load.wait()
        span = pl.ds(h * half * rows, half * rows)
        p, t = press[span], heat[span]
        liquid = flag[span] == 1
        r = inverse(field_v[0, span])
        rt = inverse(t)
        ratio_pt = p * rt
        g = ratio_pt * rt
        beta = field_v[1, span] * r
        gr = g * r
        big_a = gr * r * field_v[2, span]
        big_b = ratio_pt * beta
        z = jnp.where(liquid, big_b + 0.01, 1.0 + big_b)
        floor = big_b + 0.01
        c2 = big_b - 1.0
        c1 = big_a - 3.0 * big_b * big_b - 2.0 * big_b
        c0 = big_b * big_b + big_b * big_b * big_b - big_a * big_b
        twice = 2.0 * c2
        for _ in range(NEWT):
            value = ((z + c2) * z + c1) * z + c0
            incline = (3.0 * z + twice) * z + c1
            z = jnp.maximum(z - value * inverse(jnp.maximum(incline, 0.1)), floor)
        log_ratio = jnp.log(
            (z + (1.0 + ROOT_TWO) * big_b) * inverse(z + (1.0 - ROOT_TWO) * big_b)
        )
        lb = log_ratio * inverse(ROOT_TWO * big_b)
        e0 = jnp.log(z - big_b)
        e1 = (z - 1.0 + 0.5 * big_a * lb) * inverse(beta)
        e2 = gr * lb
        mob = ratio_pt * inverse(z * jnp.where(liquid, visc[1], visc[0]))
        mob_out[span] = mob
        field_v[0, span] = e0
        field_v[1, span] = e1
        field_v[2, span] = e2
        field_v[3, span] = mob * r
        for x in range(h * half * per, (h + 1) * half * per):
            span = pl.ds(x * ny, ny)
            e0, e1, e2, mr = (field_v[k, span].reshape(shape3) for k in range(4))
            for i in range(nc):
                value = table_v[2, i] * e1 - e0 - psi_v[i, span].reshape(shape3) * e2
                lnphi_v[i, span] = value.reshape(ny, LANES).astype(BF16)
                carried = (mr * amount_v[i, span].reshape(shape3)).reshape(ny, LANES)
                carried_out[i, pl.ds(MARGIN + x * ny, ny)] = carried
        span = pl.ds(h * half * rows, half * rows)
        stores.append(go(lnphi_v.at[:, span], lnphi_out.at[:, span], out_sems.at[h]))

    perm_load.wait()
    odd_g = lax.axis_index(axes[0]) % 2 == 1
    odd_s = lax.axis_index(axes[1]) % 2 == 1
    for k in range(edge_x_out.shape[0]):
        at_low = odd_g if k == 0 else jnp.logical_not(odd_g)
        start = pl.multiple_of(jnp.where(at_low, 0, (nx - 1) * ny), ny)
        for i in range(nc):
            edge_x_out[k, i] = carried_out[i, pl.ds(start + MARGIN, ny)]
        edge_x_out[k, nc] = press[pl.ds(start, ny)]
        edge_x_out[k, nc + 1] = perm[pl.ds(start, ny)]
    for i in range(nc + 2):
        source = carried_out.at[i] if i < nc else press if i == nc else perm
        skip = MARGIN if i < nc else 0
        low = source[pl.ds(skip, nx, stride=ny)]
        high = source[pl.ds(skip + ny - 1, nx, stride=ny)]
        edge_ya_out[i] = jnp.where(odd_s, low, high)
        edge_yb_out[i] = jnp.where(odd_s, high, low)

    row_hot, lane_hot = place_hots(loc[...], nx * ny)
    lane_hot = hot(lane_hot)

    def cells_of(field):
        return jnp.sum(jnp.where(row_hot, mat_hot(field, lane_hot), 0.0), axis=0, keepdims=True)

    p_cell = cells_of(press[...])
    pcell_out[...] = p_cell
    weight = strength[...] * cells_of(mob_out[...])
    segments = own_press.shape[1]
    perfs = loc.shape[1]
    place_of = iota((LANES, perfs), 0)
    sums = jnp.where(place_of == seg[...], weight, 0.0)
    sums += jnp.where(place_of == seg[...] + segments, weight * (p_cell - 1.0), 0.0)
    slot_hot = slot_hot_of(member[...], place[...])
    shift = hot(iota((segments, LANES), 0) + 2 * segments == iota((segments, LANES), 1))
    part_out[...] = hot_mat_nt(slot_hot.astype(BF16), sums) + mat_hot(own_press[...], shift)
    for copy in stores:
        copy.wait()


def flux_kernel(
    nx,
    ny,
    axes,
    many_x,
    carried,
    press,
    perm,
    pore,
    flag,
    mob,
    old,
    edge_ya,
    edge_yb,
    well_rows,
    loc,
    member,
    seg,
    strength,
    place,
    pcell,
    consts,
    own_press,
    order,
    exit_press,
    friction,
    *rest,
):
    edge_x, (resid_out, well_out, y_v, res_v, out_sems) = rest[:many_x], rest[many_x:]
    nc = carried.shape[0]
    g, s = lax.axis_index(axes[0]), lax.axis_index(axes[1])
    ng, ns = lax.axis_size(axes[0]), lax.axis_size(axes[1])
    odd_g, odd_s = g % 2 == 1, s % 2 == 1
    has_low_y, has_high_y = s > 0, s < ns - 1
    has_low_x, has_high_x = g > 0, g < ng - 1

    for i in range(nc + 2):
        a, b = edge_ya[i], edge_yb[i]
        low, high = jnp.where(odd_s, a, b), jnp.where(odd_s, b, a)
        if i == nc + 1:
            low, high = jnp.where(has_low_y, low, 0.0), jnp.where(has_high_y, high, 0.0)
        y_v[0, i] = low
        y_v[1, i] = high

    def side_x(i, high):
        if many_x == 1:
            return edge_x[0][i]
        return jnp.where(odd_g != high, edge_x[0][i], edge_x[1][i])

    row_hot, lane_hot = place_hots(loc[...], nx * ny)
    slot_hot = slot_hot_of(member[...], place[...])
    segments = own_press.shape[1]
    gathered = well_rows[...]
    seg_hot = hot(iota((LANES, loc.shape[1]), 0) == seg[...] + 2 * segments)
    p_seg = jnp.sum(mat_hot(gathered, seg_hot) * slot_hot, axis=0, keepdims=True)
    push = strength[...] * (pcell[...] - p_seg)
    flows = jnp.concatenate(
        [
            jnp.where(lane_hot, jnp.maximum(push, 0.0), 0.0),
            jnp.where(lane_hot, jnp.minimum(push, 0.0), 0.0),
        ],
        axis=0,
    )
    spread = hot_mat_nt(hot(row_hot), flows, 2)

    own = jnp.sum(gathered, axis=0, keepdims=True)
    well_p = own_press[...]
    rate = own[:, segments : 2 * segments] - (well_p - 1.0) * own[:, :segments]
    order_hot = hot(iota((segments, segments), 0) == order[...])
    both = mat_hot(jnp.concatenate([rate, well_p], axis=0), order_hot)
    upper = hot(iota((segments, segments), 0) <= iota((segments, segments), 1))
    running = mat_hot(both[0:1], upper)
    press_ord = both[1:2]
    after = hot(iota((segments, segments), 0) == iota((segments, segments), 1) + 1)
    last = iota((1, segments), 1) == segments - 1
    nexts = jnp.where(last, exit_press[...], mat_hot(press_ord, after))
    res_ord = press_ord - nexts - friction[...] * running * jnp.abs(running)
    well_out[...] = sum(mat_nt(piece, order_hot) for piece in pieces_of(res_ord, 3))

    lane = iota((ny, LANES), 1)
    row = iota((ny, LANES), 0)
    first, final = row == 0, row == ny - 1

    def const(k):
        return jnp.concatenate([consts[k]] * (ny // SUBLANES), axis=0)

    stores = []
    for x in range(nx):
        rows = pl.ds(x * ny, ny)
        p_a, k_a = press[rows], perm[rows]
        twice_k = 2.0 * k_a

        def face(p_b, k_b, axis):
            t = const(nc + axis) * (twice_k * k_b) * inverse(k_a + k_b)
            flow = t * (p_a - p_b)
            return jnp.maximum(flow, 0.0), jnp.minimum(flow, 0.0)

        def other_x(field, i, high):
            at = x + 1 if high else x - 1
            return field[pl.ds(at * ny, ny)] if 0 <= at < nx else side_x(i, high)

        def other_y(field, i, high):
            if high:
                return jnp.where(final, y_v[1, i, pl.ds(x, 1)], pltpu.roll(field, ny - 1, 0))
            return jnp.where(first, y_v[0, i, pl.ds(x, 1)], pltpu.roll(field, 1, 0))

        centre = pore[rows] * jnp.where(flag[rows] == 1, const(nc + 4), const(nc + 3))
        centre += spread[x * ny : (x + 1) * ny, :LANES]
        ins = []
        for high in (True, False):
            p_b, k_b = other_x(press, nc, high), other_x(perm, nc + 1, high)
            if x == nx - 1 and high:
                k_b = jnp.where(has_high_x, k_b, 0.0)
            if x == 0 and not high:
                k_b = jnp.where(has_low_x, k_b, 0.0)
            ins.append(face(p_b, k_b, 0))
        for high in (True, False):
            ins.append(face(other_y(p_a, nc, high), other_y(k_a, nc + 1, high), 1))
        for shift, edge in ((LANES - 1, LANES - 1), (1, 0)):
            k_b = jnp.where(lane == edge, 0.0, pltpu.roll(k_a, shift, 1))
            ins.append(face(pltpu.roll(p_a, shift, 1), k_b, 2))
        for out, _ in ins:
            centre += out
        ins = [into for _, into in ins]
        pushed = mob[rows] * spread[x * ny : (x + 1) * ny, LANES:]
        for i in range(nc):
            base = MARGIN + x * ny
            c = carried[i, pl.ds(base, ny)]
            value = centre * c - old[i, rows] + const(i) * pushed
            for k, high in ((0, True), (1, False)):
                at = x + 1 if high else x - 1
                inside = 0 <= at < nx
                c_b = carried[i, pl.ds(MARGIN + at * ny, ny)] if inside else side_x(i, high)
                value += ins[k] * c_b
            up, down = carried[i, pl.ds(base + 1, ny)], carried[i, pl.ds(base - 1, ny)]
            value += ins[2] * jnp.where(final, y_v[1, i, pl.ds(x, 1)], up)
            value += ins[3] * jnp.where(first, y_v[0, i, pl.ds(x, 1)], down)
            value += ins[4] * pltpu.roll(c, LANES - 1, 1)
            value += ins[5] * pltpu.roll(c, 1, 1)
            res_v[i, rows] = value
        copy = pltpu.make_async_copy(res_v.at[:, rows], resid_out.at[:, rows], out_sems.at[x])
        copy.start()
        stores.append(copy)
    for copy in stores:
        copy.wait()


def swaps_of(count, other):
    pairs = [(i, i + 1) for i in range(1 if other else 0, count - 1, 2)]
    return pairs + [(b, a) for a, b in pairs]


def per_device(
    amount,
    press,
    heat,
    flag,
    perm,
    pore,
    old,
    trans,
    visc,
    crit,
    attract,
    covol,
    slope,
    coupling,
    inject,
    locale,
    member,
    seg,
    strength,
    place,
    order,
    seg_press,
    exit_press,
    friction,
):
    axes = ("grp", "sub")
    nc, nx, ny, nz = amount.shape
    ng, ns = lax.axis_size("grp"), lax.axis_size("sub")
    rows = nx * ny
    perfs = locale.shape[0]
    wells, segments = place.shape[1], seg_press.shape[1]
    flat = lambda a: a.reshape(a.shape[:-3] + (rows, nz))
    line = lambda a: a.reshape(1, perfs)
    vm = pl.BlockSpec(memory_space=pltpu.VMEM)
    hbm = pl.BlockSpec(memory_space=pltpu.HBM)
    many_x = 1 if ng == 2 else 2

    amount, old = flat(amount), flat(old)
    press, heat, flag, perm, pore = (flat(a) for a in (press, heat, flag, perm, pore))
    locale, member, seg, strength = (line(a) for a in (locale, member, seg, strength))
    exit_press, friction = exit_press.reshape(1, 1), friction.reshape(1, 1)

    sources = (
        visc, crit, attract, covol, slope, trans, inject,
        coupling, locale, member, seg, strength, place, seg_press,
        heat, press, flag, perm,
    )
    kept = [
        pltpu.SMEM(a.shape, a.dtype) if a.ndim == 1 else pltpu.VMEM(a.shape, a.dtype)
        for a in sources
    ]
    in_hbm = lambda a: pltpu.with_memory_space_constraint(a, pltpu.HBM)

    lnphi, carried, mob, edge_x, edge_ya, edge_yb, part, pcell, consts = pl.pallas_call(
        functools.partial(phase_kernel, nx, ny, axes),
        out_shape=(
            jax.ShapeDtypeStruct((nc, rows, nz), BF16),
            jax.ShapeDtypeStruct((nc, rows + 2 * MARGIN, nz), F32),
            jax.ShapeDtypeStruct((rows, nz), F32),
            jax.ShapeDtypeStruct((many_x, nc + 2, ny, nz), F32),
            jax.ShapeDtypeStruct((nc + 2, nx, nz), F32),
            jax.ShapeDtypeStruct((nc + 2, nx, nz), F32),
            jax.ShapeDtypeStruct((wells, LANES), F32),
            jax.ShapeDtypeStruct((1, perfs), F32),
            jax.ShapeDtypeStruct((nc + 8, SUBLANES, LANES), F32),
        ),
        in_specs=[hbm] * (1 + len(sources)),
        out_specs=(hbm,) + (vm,) * 8,
        scratch_shapes=[
            *kept,
            pltpu.VMEM((nc, rows, nz), F32),
            pltpu.VMEM((3 * nc * ny, nx * nz), BF16),
            pltpu.VMEM((nc, rows, nz), F32),
            pltpu.VMEM((nc, rows, nz), BF16),
            pltpu.VMEM((4, rows, nz), F32),
            pltpu.VMEM((3, nc, SUBLANES, LANES), F32),
            pltpu.SemaphoreType.DMA((len(sources),)),
            pltpu.SemaphoreType.DMA((nx // 2,)),
            pltpu.SemaphoreType.DMA((2,)),
        ],
        compiler_params=pltpu.CompilerParams(vmem_limit_bytes=VMEM_LIMIT),
        name="phase",
    )(in_hbm(amount), *(in_hbm(a) for a in sources))

    well_rows = lax.all_to_all(part, "sub", split_axis=0, concat_axis=0, tiled=True)
    got_x = [lax.ppermute(edge_x[k], "grp", swaps_of(ng, k == 1)) for k in range(many_x)]
    got_yb = lax.ppermute(edge_yb, "sub", swaps_of(ns, True))
    got_ya = lax.ppermute(edge_ya, "sub", swaps_of(ns, False))

    resid, well = pl.pallas_call(
        functools.partial(flux_kernel, nx, ny, axes, many_x),
        out_shape=(
            jax.ShapeDtypeStruct((nc, rows, nz), F32),
            jax.ShapeDtypeStruct((1, segments), F32),
        ),
        in_specs=[vm] * (21 + many_x),
        out_specs=(hbm, vm),
        scratch_shapes=[
            pltpu.VMEM((2, nc + 2, nx, nz), F32),
            pltpu.VMEM((nc, rows, nz), F32),
            pltpu.SemaphoreType.DMA((nx,)),
        ],
        compiler_params=pltpu.CompilerParams(vmem_limit_bytes=VMEM_LIMIT),
        name="flux",
    )(
        carried, press, perm, pore, flag, mob, old, got_ya, got_yb, well_rows,
        locale, member, seg, strength, place, pcell,
        consts, seg_press, order, exit_press, friction, *got_x,
    )
    block = (nc, nx, ny, nz)
    return resid.reshape(block), lnphi.reshape(block), well


def solution(mesh):
    cells, parts = P("grp", "sub", None), P(None, "grp", "sub", None)
    listed = P(("grp", "sub"))
    row = P(("grp", "sub"), None)
    in_specs = (
        (parts,) + (cells,) * 5 + (parts,) + (P(),) * 8
        + (listed, row, listed, listed, P("grp", None), row, row, listed, listed)
    )
    return jax.shard_map(
        per_device, mesh=mesh, in_specs=in_specs, out_specs=(parts, parts, row), check_vma=False
    )
```

time: 73.8 us -> 27 us (0.37)
  blocking collectives: 55.9 us -> 0 us
  starting transfers between devices: 0 us -> 11.5 us
  local copies, waits for them, and re-layouts: 6.53 us -> 0.05 us
  waiting for transfers between devices: 0 us -> 5.05 us
  Pallas kernels: 8.87 us -> 8.05 us
    all_gather x5 -> x0, blocking collectives: 55.9 us -> none  [the longest x1 23.1 us: per_device(): all_press = lax.all_gather(seg_press, 'sub', tiled=True)]
    all_to_all x0 -> x1, starting transfers between devices: none -> 7.81 us  [per_device(): lax.all_to_all(part, 'sub', split_axis=0, concat_axis=0, tiled=True)]
    unnamed x46 -> x24, local copies, waits for them, and re-layouts: 6.53 us -> 0.05 us
    all_to_all x0 -> x1, waiting for transfers between devices: none -> 5.04 us  [per_device(): lax.all_to_all(part, 'sub', split_axis=0, concat_axis=0, tiled=True)]
    ppermute x0 -> x3, starting transfers between devices: none -> 3.66 us  [the longest x1 3 us: per_device(): lax.ppermute(edge_x[k], 'grp', swaps_of(ng, k == 1))]
    pallas_call x1, Pallas kernels: 4.44 us -> 2.55 us  [per_device(): pl.pallas_call(functools.partial(flux_kernel, nx, ny, axes, many_x), out_...]
    pallas_call x1, Pallas kernels: 4.43 us -> 5.5 us  [per_device(): pl.pallas_call(functools.partial(phase_kernel, nx, ny, axes), out_shape=(...]
  transfers between devices with their start and end apart: 0 -> 4, of which waited for: 0 -> 1; matrix products, arithmetic and copies ran while one was open for 0% -> 0% of each run, Pallas kernels for 0% -> 0%
where the time goes in v2:
time: 27 us; the launch traced here: 26.8 us
  starting transfers between devices  11.5 us (43%)
  Pallas kernels  8.05 us (30%)
  waiting for transfers between devices  5.05 us (19%)
  between operations  2.15 us (8%)
    all_to_all x1, starting transfers between devices, per_device(): lax.all_to_all(part, 'sub', split_axis=0, concat_axis=0, tiled=True)  7.81 us
    pallas_call x1, Pallas kernels, per_device(): pl.pallas_call(functools.partial(phase_kernel, nx, ny, axes), out_shape=(...  5.5 us
    all_to_all x1, waiting for transfers between devices, per_device(): lax.all_to_all(part, 'sub', split_axis=0, concat_axis=0, tiled=True)  5.04 us
    ppermute x1, starting transfers between devices, per_device(): lax.ppermute(edge_x[k], 'grp', swaps_of(ng, k == 1))  3 us
    pallas_call x1, Pallas kernels, per_device(): pl.pallas_call(functools.partial(flux_kernel, nx, ny, axes, many_x), out_...  2.55 us
    ppermute x1, starting transfers between devices, per_device(): got_yb = lax.ppermute(edge_yb, 'sub', swaps_of(ns, True))  0.65 us
  transfers between devices with their start and end apart: 4, of which 1 were waited for; matrix products, arithmetic and copies ran while one was open for 0% of the time, Pallas kernels for 0%

profile of v2, /device:TPU:0, one launch (start us, length us, event | category | flops | bytes accessed | tf_op | source)
XLA Modules:
  0.0 26.8 jit_solution(18093161029649728104)
XLA Ops:
  0.6 0.0 copy-start.10
  0.6 0.0 copy-start.9
  0.7 0.0 copy-start.8
  0.7 0.0 copy-start.7
  0.7 0.0 copy-start.6
  0.7 0.0 copy-start.5
  0.7 0.0 copy-start.3
  0.7 0.0 copy-start.2
  0.7 0.0 copy-start.1
  0.7 0.0 copy-start.11
  0.7 0.0 copy-start
  0.7 0.0 copy-start.4
  0.8 5.5 %phase.1 = (bf16[16,128,128]{2,1,0:T(8,128)(2,1)}, f32[16,144,128]{2,1,0:T(8,128)S(1)}, f32[128,128]{1,0:T(8,128)S(1)}, f32[1,18,16,128]{3,2,1,0:T(8,128)S(1)}, ...) custom-call(f32[16,128,128]{2,1,0:T(8,128)} %bitcast.40, ...), custom_call_target="tpu_custom_call" | custom-call | tf_op jit(solution)/shard_map/phase/pallas_call | solution.py:474
  6.3 3.0 %collective-permute-start.2 = (f32[18,16,128]{2,1,0:T(8,128)S(1)}, f32[18,16,128]{2,1,0:T(8,128)S(1)}, u32[]{:S(2)}, u32[]{:S(2)}) collective-permute-start(f32[18,16,128]{2,1,0:T(8,128)S(1)} %bitcast.39), channel_id=1, source_target_pairs={{0,16},{16,0},{1,17},{17,1},{2,18},{18,2},{3,19},{19,3},{4,20},{20... | collective-permute-start | bytes 442376 | tf_op jit(solution)/shard_map/ppermute | solution.py:506
  9.3 0.0 collective-permute-start
  9.3 0.7 %collective-permute-start.1 = (f32[18,8,128]{2,1,0:T(8,128)S(1)}, f32[18,8,128]{2,1,0:T(8,128)S(1)}, u32[]{:S(2)}, u32[]{:S(2)}) collective-permute-start(f32[18,8,128]{2,1,0:T(8,128)S(1)} %get-tuple-element.17), channel_id=1, source_target_pairs={{1,2},{3,4},{5,6},{7,8},{9,10},{11,12},{13,14},{2,1},{4,3},{6,5},{... | collective-permute-start | bytes 221192 | tf_op jit(solution)/shard_map/ppermute | solution.py:507
  9.9 7.8 %all-to-all-start = ((f32[16,1,128]{2,1,0:T(1,128)}), f32[16,1,128]{2,1,0:T(1,128)S(1)}, u32[]{:S(2)}, u32[]{:S(2)}) async-start(f32[16,1,128]{2,1,0:T(1,128)} %bitcast.12), calls=%async_computation | async-start | bytes 16384 | tf_op jit(solution)/shard_map/all_to_all | solution.py:505
  19.1 5.0 %all-to-all-done = f32[16,1,128]{2,1,0:T(1,128)S(1)} async-done(((f32[16,1,128]{2,1,0:T(1,128)}), f32[16,1,128]{2,1,0:T(1,128)S(1)}, u32[]{:S(2)}, u32[]{:S(2)}) %all-to-all-start) | async-done | bytes 8224 | tf_op jit(solution)/shard_map/all_to_all | solution.py:505
  24.1 0.0 collective-permute-done.edge_ya
  24.1 0.0 collective-permute-done.1.edge_yb
  24.1 0.0 collective-permute-done.2.rest_0_
  24.1 0.0 copy-done.10
  24.1 0.0 copy-done.9
  24.1 0.0 copy-done.8
  24.1 0.0 copy-done.7
  24.1 0.0 copy-done.6
  24.2 0.0 copy-done.5
  24.2 0.0 copy-done.3
  24.2 0.0 copy-done.2
  24.2 0.0 copy-done.1
  24.2 0.0 copy-done.11
  24.2 0.0 copy-done
  24.2 0.0 copy-done.4
  24.2 2.5 %flux.1 = (f32[16,128,128]{2,1,0:T(8,128)}, f32[1,32]{1,0:T(1,128)}) custom-call(f32[16,144,128]{2,1,0:T(8,128)S(1)} %get-tuple-element.14.carried, f32[128,128]{1,0:T(8,128)S(1)} %bitcast.24, f32[128,128]{1,0:T(8,128)S(1)} %bitcast.28, f32[128,128]{1,0:T(8,128)S(1)} %bitcast.29, s32[128,128]{1,0:T(8,128)S(1)} %bitcast.26, ...), custom_call_target="tpu_custom_call" | custom-call | tf_op jit(solution)/shard_map/flux/pallas_call | solution.py:510
Async XLA Ops:
  0.6 23.5 %copy-start.10 = (f32[1,32]{1,0:T(1,128)S(1)}, f32[1,32]{1,0:T(1,128)}, u32[]{:S(2)}) copy-start(f32[1,32]{1,0:T(1,128)} %own_press.1) | copy-start | bytes 388
  0.6 23.5 %copy-start.9 = (s32[1,16]{1,0:T(1,128)S(1)}, s32[1,16]{1,0:T(1,128)}, u32[]{:S(2)}) copy-start(s32[1,16]{1,0:T(1,128)} %place.1) | copy-start | bytes 196
  0.7 23.5 %copy-start.8 = (f32[256]{0:T(256)S(1)}, f32[256]{0:T(256)}, u32[]{:S(2)}) copy-start(f32[256]{0:T(256)} %param.42) | copy-start | bytes 3076
  0.7 23.5 %copy-start.7 = (s32[256]{0:T(256)S(1)}, s32[256]{0:T(256)}, u32[]{:S(2)}) copy-start(s32[256]{0:T(256)} %param.41) | copy-start | bytes 3076
  0.7 23.5 %copy-start.6 = (s32[256,1]{0,1:T(1,128)S(1)}, s32[256,1]{0,1:T(1,128)}, u32[]{:S(2)}) copy-start(s32[256,1]{0,1:T(1,128)} %param.40) | copy-start | bytes 3076
  0.7 23.5 %copy-start.5 = (s32[256]{0:T(256)S(1)}, s32[256]{0:T(256)}, u32[]{:S(2)}) copy-start(s32[256]{0:T(256)} %param.39) | copy-start | bytes 3076
  0.7 23.5 %copy-start.3 = (f32[8,16,128]{2,1,0:T(8,128)S(1)}, f32[8,16,128]{2,1,0:T(8,128)}, u32[]{:S(2)}) copy-start(f32[8,16,128]{2,1,0:T(8,128)} %param.28) | copy-start | bytes 196612
  0.7 23.5 %copy-start.2 = (s32[8,16,128]{2,1,0:T(8,128)S(1)}, s32[8,16,128]{2,1,0:T(8,128)}, u32[]{:S(2)}) copy-start(s32[8,16,128]{2,1,0:T(8,128)} %param.27) | copy-start | bytes 196612
  0.7 23.5 %copy-start.1 = (f32[8,16,128]{2,1,0:T(8,128)S(1)}, f32[8,16,128]{2,1,0:T(8,128)}, u32[]{:S(2)}) copy-start(f32[8,16,128]{2,1,0:T(8,128)} %param.25) | copy-start | bytes 196612
  0.7 23.5 %copy-start.11 = (s32[1,32]{1,0:T(1,128)S(1)}, s32[1,32]{1,0:T(1,128)}, u32[]{:S(2)}) copy-start(s32[1,32]{1,0:T(1,128)} %order.1) | copy-start | bytes 388
  0.7 23.5 %copy-start = (f32[16,8,16,128]{3,2,1,0:T(8,128)S(1)}, f32[16,8,16,128]{3,2,1,0:T(8,128)}, u32[]{:S(2)}) copy-start(f32[16,8,16,128]{3,2,1,0:T(8,128)} %param.30) | copy-start | bytes 3145732
  0.7 23.5 %copy-start.4 = (f32[8,16,128]{2,1,0:T(8,128)S(1)}, f32[8,16,128]{2,1,0:T(8,128)}, u32[]{:S(2)}) copy-start(f32[8,16,128]{2,1,0:T(8,128)} %param.29) | copy-start | bytes 196612
  6.3 17.8 %collective-permute-start.2 = (f32[18,16,128]{2,1,0:T(8,128)S(1)}, f32[18,16,128]{2,1,0:T(8,128)S(1)}, u32[]{:S(2)}, u32[]{:S(2)}) collective-permute-start(f32[18,16,128]{2,1,0:T(8,128)S(1)} %bitcast.39), channel_id=1, source_target_pairs={{0,16},{16,0},{1,17},{17,1},{2,18},{18,2},{3,19},{19,3},{4,20},{20... | collective-permute-start | bytes 442376 | tf_op jit(solution)/shard_map/ppermute | solution.py:506
  9.3 14.8 %collective-permute-start = (f32[18,8,128]{2,1,0:T(8,128)S(1)}, f32[18,8,128]{2,1,0:T(8,128)S(1)}, u32[]{:S(2)}, u32[]{:S(2)}) collective-permute-start(f32[18,8,128]{2,1,0:T(8,128)S(1)} %get-tuple-element.16), channel_id=1, source_target_pairs={{0,1},{2,3},{4,5},{6,7},{8,9},{10,11},{12,13},{14,15},{1,0},{3,2},... | collective-permute-start | bytes 221192 | tf_op jit(solution)/shard_map/ppermute | solution.py:508
  9.3 14.8 %collective-permute-start.1 = (f32[18,8,128]{2,1,0:T(8,128)S(1)}, f32[18,8,128]{2,1,0:T(8,128)S(1)}, u32[]{:S(2)}, u32[]{:S(2)}) collective-permute-start(f32[18,8,128]{2,1,0:T(8,128)S(1)} %get-tuple-element.17), channel_id=1, source_target_pairs={{1,2},{3,4},{5,6},{7,8},{9,10},{11,12},{13,14},{2,1},{4,3},{6,5},{... | collective-permute-start | bytes 221192 | tf_op jit(solution)/shard_map/ppermute | solution.py:507
  9.9 14.2 %all-to-all-start = ((f32[16,1,128]{2,1,0:T(1,128)}), f32[16,1,128]{2,1,0:T(1,128)S(1)}, u32[]{:S(2)}, u32[]{:S(2)}) async-start(f32[16,1,128]{2,1,0:T(1,128)} %bitcast.12), calls=%async_computation | async-start | bytes 16384 | tf_op jit(solution)/shard_map/all_to_all | solution.py:505
